TPU v7x, 128 devices: a whole 4x4x4 slice. The times are simulated.
128 devices in a mesh: front: 32 (over z, y, x_hi), row: 2 (over core), col: 2 (over x_lo).
Axes of the slice: x: 4 (x_hi: 2, x_lo: 2; x = x_hi * 2 + x_lo), y: 4, z: 4, core: 2. Of those that a mesh axis runs over, the one named last changes fastest.
Arguments:
- bounds: int32 [32], P('front'), may hold values from 3072 to 5120, as said below
- block_map: int32 [32, 40], P('front', 'row'), may hold values from 0 to 1535, as said below
- pivot_inverse: bfloat16 [32, 1024, 1024], P('front', 'col', 'row'), may hold values from -0.1875 to 0.1875
- upper_block: bfloat16 [32, 1024, 5120], P('front', 'row', 'col'), may hold values from -0.078125 to 0.078125
- lower_block: bfloat16 [32, 5120, 1024], P('front', 'row', 'col'), may hold values from -0.1875 to 0.1875
- trailing_block: bfloat16 [32, 5120, 5120], P('front', 'row', 'col'), may hold values from -0.078125 to 0.078125
- sketch: bfloat16 [5120, 512], P('col'), may hold values from -6 to 6
- basis: bfloat16 [32, 6144, 512], P('front', 'row'), may hold values from -0.078125 to 0.078125
Outputs:
- coefficients: float32 [32, 512, 512], P('front', None, 'col')
- residual: float32 [32, 6144, 512], P('front', 'row', 'col')
Inputs may be any that keep to these rules, and one draw needn't show every extreme that they name: `bounds`: each is a multiple of 128; some front has exactly 5120. `block_map`: entries for blocks at or beyond a front's boundary are ignored. Within one front all entries are distinct. Owner (g, r) holds parent blocks g * 48 + r * 24 to g * 48 + (r + 1) * 24 - 1; an entry held by the device at index r of row names a block of an owner with the same r. Among the 20 entries held by one device, at most 1 name blocks of one owner, and some device has exactly 1 for some owner.
All inputs are finite; a program needn't handle non-finite values.
Results may differ from a plain program's by a relative error of at most 0.0042.
Values may be sent and summed in bfloat16 or wider, within the bound.
A program may use at most 128 MiB of HBM per device.

v0:
```python
import jax
import jax.numpy as jnp
from jax import lax
from jax.sharding import PartitionSpec as P

BLOCK = 128


def split_up(shard, dim, peers):
    before, after = (shard.shape[:dim], shard.shape[dim + 1 :])
    return jnp.moveaxis(shard.reshape(*before, peers, -1, *after), dim, 0)


def sum_at_owner(shard, axis, dim):
    peers = lax.axis_size(axis)
    pieces = lax.all_to_all(split_up(shard, dim, peers), axis, 0, 0, tiled=True)
    return jnp.sum(pieces, axis=0)


def laid_out(pieces, dim):
    pieces = jnp.moveaxis(pieces, 0, dim)
    shape = pieces.shape
    return pieces.reshape(*shape[:dim], shape[dim] * shape[dim + 1], *shape[dim + 2 :])


def copy_for_each(shard, axis):
    peers = lax.axis_size(axis)
    return lax.all_to_all(
        jnp.broadcast_to(shard[None], (peers, *shard.shape)), axis, 0, 0, tiled=True
    )


def gathered_copies(shard, axis, dim):
    return laid_out(copy_for_each(shard, axis), dim)


def taken_together(shard, axis):
    everything = copy_for_each(shard, axis)
    return jnp.sum(everything, axis=0)


def extend_add(blocks, targets, live_rows, per_device):
    dest_count = lax.axis_size("front")
    row_count = lax.axis_size("row")
    capacity = (blocks.shape[0] + dest_count - 1) // dest_count
    block_height = blocks.shape[1]
    lane_width = blocks.shape[2]
    destination = targets // (row_count * per_device)
    local_block = targets % per_device
    dest_hits = (
        destination[:, None] == jnp.arange(dest_count, dtype=jnp.int32)[None, :]
    ) & live_rows[:, None]
    dest_counts = dest_hits.astype(jnp.int32)
    earlier = jnp.cumsum(dest_counts, axis=0) - dest_counts
    slot_rank = jnp.sum(earlier * dest_counts, axis=1)
    slot_index = destination * capacity + slot_rank
    chosen = (
        slot_index[None, :] == jnp.arange(dest_count * capacity, dtype=jnp.int32)[:, None]
    ) & live_rows[None, :]
    outgoing = jnp.einsum(
        "ps,sbw->pbw", chosen.astype(jnp.float32), blocks, precision=lax.Precision.HIGHEST
    )
    slot_tags = jnp.where(
        jnp.any(chosen, axis=1),
        jnp.sum(jnp.where(chosen, local_block[None, :], 0), axis=1),
        per_device,
    )
    incoming, incoming_tags = (
        lax.all_to_all(
            outgoing.reshape(dest_count, capacity, block_height, lane_width),
            "front",
            split_axis=0,
            concat_axis=0,
            tiled=True,
        ),
        lax.all_to_all(
            slot_tags.reshape(dest_count, capacity),
            "front",
            split_axis=0,
            concat_axis=0,
            tiled=True,
        ),
    )
    incoming = incoming.reshape(-1, block_height, lane_width)
    incoming_tags = incoming_tags.reshape(-1)
    owner_hits = (
        jnp.arange(per_device, dtype=jnp.int32)[:, None] == incoming_tags[None, :]
    ).astype(jnp.float32)
    return jnp.einsum("qs,sbw->qbw", owner_hits, incoming, precision=lax.Precision.HIGHEST)


def body(bounds, block_map, pivot_inverse, upper_block, lower_block, trailing_block, sketch, basis):
    row_index = lax.axis_index("row")
    col_index = lax.axis_index("col")
    col_width = sketch.shape[0]
    block_rows = block_map.shape[1]
    col_positions = col_index * col_width + jnp.arange(col_width, dtype=jnp.int32)
    block_starts = (row_index * block_rows + jnp.arange(block_rows, dtype=jnp.int32)) * BLOCK
    boundary = bounds[0]
    masked = sketch * (col_positions < boundary).astype(jnp.bfloat16)[:, None]
    upper_term = jnp.dot(upper_block[0], masked, preferred_element_type=jnp.float32)
    pivot_cols = sum_at_owner(upper_term, "col", 1).astype(jnp.bfloat16)
    pivot_rows = gathered_copies(pivot_cols, "col", 1)
    solved = taken_together(
        jnp.dot(pivot_inverse[0], pivot_rows, preferred_element_type=jnp.float32), "row"
    ).astype(jnp.bfloat16)
    combined = jnp.dot(trailing_block[0], masked, preferred_element_type=jnp.float32) - jnp.dot(
        lower_block[0], solved, preferred_element_type=jnp.float32
    )
    combined = sum_at_owner(combined, "col", 1)
    sketched = combined.reshape(block_rows, BLOCK, combined.shape[1])
    alive_rows = block_starts < boundary
    per_device = basis.shape[1] // BLOCK
    parent = extend_add(sketched, block_map.reshape(-1), alive_rows, per_device)
    sketch_rows = parent.reshape(-1, parent.shape[2])
    local_basis = basis[0]
    coeff_part = lax.dot_general(
        local_basis,
        sketch_rows.astype(jnp.bfloat16),
        (((0,), (0,)), ((), ())),
        preferred_element_type=jnp.float32,
    )
    coefficients = taken_together(coeff_part, "row")
    residual = sketch_rows - jnp.dot(
        local_basis, coefficients.astype(jnp.bfloat16), preferred_element_type=jnp.float32
    )
    return (coefficients[None], residual[None])


def solution(mesh):
    placed = (
        P("front"),
        P("front", "row"),
        P("front", "col", "row"),
        P("front", "row", "col"),
        P("front", "row", "col"),
        P("front", "row", "col"),
        P("col", None),
        P("front", "row", None),
    )
    return jax.shard_map(
        body,
        mesh=mesh,
        in_specs=placed,
        out_specs=(P("front", None, "col"), P("front", "row", "col")),
        check_vma=False,
    )
```

profile of v0, /device:TPU:1, one launch (start us, length us, event | category | flops | bytes accessed | tf_op | source)
XLA Modules:
  0.0 261.1 jit_solution(7289426732576480038)
XLA Ops:
  1.5 4.7 %fusion.13 = f32[512,512]{1,0:T(8,128)S(1)} fusion(bf16[1,512,2560]{2,1,0:T(8,128)(2,1)} %param.11, bf16[2560,512]{1,0:T(8,128)(2,1)} %param.14, bf16[2560]{0:T(1024)(128)(2,1)S(1)} %fusion.36), kind=kOutput, calls=%fused_computation.15 | convolution fusion | flops 1343488000 | bytes 6296576 | tf_op jit(solution)/shard_map/dot_general | solution.py:101
  6.1 16.7 %all_to_all.36 = f32[2,512,256]{1,2,0:T(8,128)} all-to-all(f32[2,512,256]{1,2,0:T(8,128)S(1)} %bitcast.88), channel_id=1, replica_groups=mesh['front'=32,'row'=2,'col'=2] {'col'}, dimensions={0} | all-to-all | bytes 2097152 | tf_op jit(solution)/shard_map/all_to_all | solution.py:16
  22.8 1.3 reduce_sum.59
  24.1 0.8 broadcast_in_dim.32
  25.0 4.2 %all-to-all-start.2 = ((bf16[2,512,256]{1,2,0:T(8,128)(2,1)}), bf16[2,512,256]{1,2,0:T(8,128)(2,1)}, u32[]{:S(2)}, u32[]{:S(2)}) async-start(bf16[2,512,256]{1,2,0:T(8,128)(2,1)} %broadcast_in_dim.32), calls=%async_computation.2 | async-start | bytes 1048576 | tf_op jit(solution)/shard_map/all_to_all | solution.py:28
  29.2 13.2 %fusion = f32[512,2560]{1,0:T(8,128)} fusion(bf16[1,2560,2560]{2,1,0:T(8,128)(2,1)} %param.13, bf16[2560,512]{1,0:T(8,128)(2,1)} %param.14, bf16[2560]{0:T(1024)(128)(2,1)S(1)} %fusion.36), kind=kOutput, calls=%fused_computation | convolution fusion | flops 6712197120 | bytes 20976640 | tf_op jit(solution)/shard_map/dot_general | solution.py:107
  42.4 2.6 %convolution_bitcast_fusion.1 = f32[512,512]{0,1:T(8,128)} fusion(bf16[512,512]{0,1:T(8,128)(2,1)} %bitcast.15, bf16[1,512,512]{2,1,0:T(8,128)(2,1)} %param.10), kind=kOutput, calls=%fused_computation.20 | convolution fusion | flops 268435456 | bytes 2097152 | tf_op jit(solution)/shard_map/dot_general | solution.py:105
  45.1 2.6 copy.43
  47.6 1.5 broadcast_in_dim.56
  49.1 7.7 %all_to_all.37 = f32[2,512,512]{2,1,0:T(8,128)} all-to-all(f32[2,512,512]{2,1,0:T(8,128)S(1)} %broadcast_in_dim.56), channel_id=1, replica_groups=mesh['front'=32,'row'=2,'col'=2] {'row'}, dimensions={0} | all-to-all | bytes 4194304 | tf_op jit(solution)/shard_map/all_to_all | solution.py:28
  56.8 2.7 %reduce_sum.60 = bf16[512,512]{1,0:T(8,128)(2,1)} reduce(f32[2,512,512]{2,1,0:T(8,128)} %all_to_all.37, f32[]{:T(128)} %constant.42.clone.1), dimensions={0}, to_apply=%region_5.6 | reduce | flops 262144 | bytes 2621444 | tf_op jit(solution)/shard_map/reduce_sum | solution.py:39
  59.5 7.3 %convolution_subtract_fusion = f32[512,2560]{1,0:T(8,128)} fusion(f32[512,2560]{1,0:T(8,128)} %fusion, bf16[1,2560,512]{2,1,0:T(8,128)(2,1)} %param.12, bf16[512,512]{1,0:T(8,128)(2,1)} %reduce_sum.60), kind=kOutput, calls=%fused_computation.2 | convolution fusion | flops 1343488000 | bytes 13631488 | tf_op jit(solution)/shard_map/dot_general | solution.py:107
  66.9 6.1 %all-to-all-start.4 = ((f32[2,2560,256]{1,2,0:T(8,128)}), f32[2,2560,256]{1,2,0:T(8,128)}, u32[]{:S(2)}, u32[]{:S(2)}) async-start(f32[2,2560,256]{1,2,0:T(8,128)} %bitcast.83), calls=%async_computation.4 | async-start | bytes 10485760 | tf_op jit(solution)/shard_map/all_to_all | solution.py:16
  73.5 0.7 copy.42
  74.2 57.7 %all-to-all-done.4 = f32[2,2560,256]{1,2,0:T(8,128)} async-done(((f32[2,2560,256]{1,2,0:T(8,128)}), f32[2,2560,256]{1,2,0:T(8,128)}, u32[]{:S(2)}, u32[]{:S(2)}) %all-to-all-start.4) | async-done | bytes 5242912 | tf_op jit(solution)/shard_map/all_to_all | solution.py:16
  132.0 10.9 %all-to-all-start = ((s32[32,1,1]{2,1,0:T(1,128)}), s32[32,1,1]{2,1,0:T(1,128)S(1)}, u32[]{:S(2)}, u32[]{:S(2)}) async-start(s32[32,1,1]{2,1,0:T(1,128)} %copy.42), calls=%async_computation | async-start | bytes 32768 | tf_op jit(solution)/shard_map/all_to_all | solution.py:76
  142.9 4.6 %reduce_sum.61 = f32[2560,256]{0,1:T(8,128)} reduce(f32[2,2560,256]{1,2,0:T(8,128)} %all-to-all-done.4, f32[]{:T(128)} %constant.42.clone.1), dimensions={0}, to_apply=%region_6.7 | reduce | flops 655360 | bytes 7864324 | tf_op jit(solution)/shard_map/reduce_sum | solution.py:17
  147.5 3.2 %copy.44 = f32[2560,256]{1,0:T(8,128)} copy(f32[2560,256]{0,1:T(8,128)} %reduce_sum.61) | data formatting | bytes 5242880 | tf_op jit(solution)/shard_map/reduce_sum | solution.py:17
  150.7 5.5 %fusion.17 = f32[32,1,128,256]{3,0,2,1:T(8,128)S(1)} fusion(f32[20,128,256]{2,1,0:T(8,128)} %bitcast.84, s32[20]{0:T(128)S(1)} %get-tuple-element.15, pred[20]{0:T(512)(128)(4,1)S(1)} %multiply_compare_fusion), kind=kOutput, calls=%fused_computation.19 | convolution fusion | flops 251659520 | bytes 6815844 | tf_op jit(solution)/shard_map/ps,sbw->pbw/dot_general | solution.py:60
  156.2 4.4 %copy.46 = f32[32,1,128,256]{3,2,1,0:T(8,128)} copy(f32[32,1,128,256]{3,0,2,1:T(8,128)S(1)} %fusion.17) | data formatting | bytes 8388608 | tf_op jit(solution)/shard_map/reshape | solution.py:70
  160.6 9.4 %all-to-all-start.5 = ((f32[32,1,128,256]{3,2,1,0:T(8,128)}), f32[32,1,128,256]{3,2,1,0:T(8,128)}, u32[]{:S(2)}, u32[]{:S(2)}) async-start(f32[32,1,128,256]{3,2,1,0:T(8,128)} %copy.46), calls=%async_computation.5 | async-start | bytes 8388608 | tf_op jit(solution)/shard_map/all_to_all | solution.py:69
  170.7 50.3 %all-to-all-done.5 = f32[32,1,128,256]{3,2,1,0:T(8,128)} async-done(((f32[32,1,128,256]{3,2,1,0:T(8,128)}), f32[32,1,128,256]{3,2,1,0:T(8,128)}, u32[]{:S(2)}, u32[]{:S(2)}) %all-to-all-start.5) | async-done | bytes 4194336 | tf_op jit(solution)/shard_map/all_to_all | solution.py:69
  221.0 7.8 %fusion.43 = (bf16[24,128,256]{2,0,1:T(8,128)(2,1)S(1)}, f32[24,128,256]{2,0,1:T(8,128)}) fusion(f32[32,1,128,256]{3,2,1,0:T(8,128)} %all-to-all-done.5, s32[32]{0:T(128)S(1)} %reduce), kind=kOutput, calls=%fused_computation.53 | convolution fusion | flops 302777088 | bytes 8913024 | tf_op jit(solution)/shard_map/qs,sbw->qbw/dot_general | solution.py:89
  229.2 1.8 fusion.22
  231.0 2.0 copy.49
  233.0 2.1 broadcast_in_dim.57
  235.1 7.4 %all-to-all-start.6 = ((f32[2,512,256]{2,1,0:T(8,128)}), f32[2,512,256]{2,1,0:T(8,128)}, u32[]{:S(2)}, u32[]{:S(2)}) async-start(f32[2,512,256]{2,1,0:T(8,128)} %broadcast_in_dim.57), calls=%async_computation.6 | async-start | bytes 2097152 | tf_op jit(solution)/shard_map/all_to_all | solution.py:28
  242.5 4.6 %copy.50 = f32[24,128,256]{2,1,0:T(8,128)} copy(f32[24,128,256]{2,0,1:T(8,128)} %get-tuple-element.17) | data formatting | bytes 6291456 | tf_op jit(solution)/shard_map/qs,sbw->qbw/dot_general | solution.py:89
  247.1 3.5 %copy.51 = f32[3072,256]{0,1:T(8,128)} copy(f32[3072,256]{1,0:T(8,128)} %bitcast.85) | data formatting | bytes 6291456 | tf_op jit(solution)/shard_map/reshape | solution.py:115
  250.7 2.1 reduce_sum.62
  252.8 4.8 %fusion.6 = f32[1,3072,256]{1,2,0:T(8,128)} fusion(f32[3072,256]{0,1:T(8,128)} %copy.51, bf16[1,3072,512]{2,1,0:T(8,128)(2,1)S(1)} %copy-done, f32[512,256]{1,0:T(8,128)} %reduce_sum.62), kind=kOutput, calls=%fused_computation.8 | convolution fusion | flops 806223872 | bytes 9961472 | tf_op jit(solution)/shard_map/dot_general | solution.py:124
  257.6 3.5 %copy.52 = f32[1,3072,256]{2,1,0:T(8,128)} copy(f32[1,3072,256]{1,2,0:T(8,128)} %fusion.6) | data formatting | bytes 6291456
  (19 shorter events, 1.6 us)
Async XLA Ops:
  0.6 228.6 %copy-start = (bf16[1,3072,512]{2,1,0:T(8,128)(2,1)S(1)}, bf16[1,3072,512]{2,1,0:T(8,128)(2,1)}, u32[]{:S(2)}) copy-start(bf16[1,3072,512]{2,1,0:T(8,128)(2,1)} %param.15) | copy-start | bytes 9437188
  25.0 17.5 %all-to-all-start.2 = ((bf16[2,512,256]{1,2,0:T(8,128)(2,1)}), bf16[2,512,256]{1,2,0:T(8,128)(2,1)}, u32[]{:S(2)}, u32[]{:S(2)}) async-start(bf16[2,512,256]{1,2,0:T(8,128)(2,1)} %broadcast_in_dim.32), calls=%async_computation.2 | async-start | bytes 1048576 | tf_op jit(solution)/shard_map/all_to_all | solution.py:28
  66.9 6.1 %copy-start.1 = (s32[1,20]{1,0:T(1,128)S(1)}, s32[1,20]{1,0:T(1,128)}, u32[]{:S(2)}) copy-start(s32[1,20]{1,0:T(1,128)} %param.9) | copy-start | bytes 244
  66.9 65.1 %all-to-all-start.4 = ((f32[2,2560,256]{1,2,0:T(8,128)}), f32[2,2560,256]{1,2,0:T(8,128)}, u32[]{:S(2)}, u32[]{:S(2)}) async-start(f32[2,2560,256]{1,2,0:T(8,128)} %bitcast.83), calls=%async_computation.4 | async-start | bytes 10485760 | tf_op jit(solution)/shard_map/all_to_all | solution.py:16
  132.0 28.7 %all-to-all-start = ((s32[32,1,1]{2,1,0:T(1,128)}), s32[32,1,1]{2,1,0:T(1,128)S(1)}, u32[]{:S(2)}, u32[]{:S(2)}) async-start(s32[32,1,1]{2,1,0:T(1,128)} %copy.42), calls=%async_computation | async-start | bytes 32768 | tf_op jit(solution)/shard_map/all_to_all | solution.py:76
  160.6 60.4 %all-to-all-start.5 = ((f32[32,1,128,256]{3,2,1,0:T(8,128)}), f32[32,1,128,256]{3,2,1,0:T(8,128)}, u32[]{:S(2)}, u32[]{:S(2)}) async-start(f32[32,1,128,256]{3,2,1,0:T(8,128)} %copy.46), calls=%async_computation.5 | async-start | bytes 8388608 | tf_op jit(solution)/shard_map/all_to_all | solution.py:69
  235.1 15.6 %all-to-all-start.6 = ((f32[2,512,256]{2,1,0:T(8,128)}), f32[2,512,256]{2,1,0:T(8,128)}, u32[]{:S(2)}, u32[]{:S(2)}) async-start(f32[2,512,256]{2,1,0:T(8,128)} %broadcast_in_dim.57), calls=%async_computation.6 | async-start | bytes 2097152 | tf_op jit(solution)/shard_map/all_to_all | solution.py:28
where the time goes:
time: 262 us; the launch traced here: 261 us
  waiting for transfers between devices  108 us (41%)
  matrix products  47.7 us (18%)
  starting transfers between devices  38.1 us (15%)
  local copies, waits for them, and re-layouts  29.3 us (11%)
  blocking collectives  24.3 us (9%)
  other arithmetic  12 us (5%)
    all_to_all x1, waiting for transfers between devices, sum_at_owner(): pieces = lax.all_to_all(split_up(shard, dim, peers), axis, 0, 0, tiled=True)  57.7 us
    all_to_all x1, waiting for transfers between devices, extend_add(): lax.all_to_all(outgoing.reshape(dest_count, capacity, block_height, lane_...  50.3 us
    all_to_all x1, blocking collectives, sum_at_owner(): pieces = lax.all_to_all(split_up(shard, dim, peers), axis, 0, 0, tiled=True)  16.7 us
    dot_general x1, matrix products, body(): jnp.dot(trailing_block[0], masked, preferred_element_type=jnp.float32)  13.2 us
    all_to_all x2, starting transfers between devices, copy_for_each(): lax.all_to_all(jnp.broadcast_to(shard[None], (peers, *shard.shape)), axis...  11.7 us
    all_to_all x1, starting transfers between devices, extend_add(): lax.all_to_all(slot_tags.reshape(dest_count, capacity), 'front', split_ax...  10.9 us
    all_to_all x1, starting transfers between devices, extend_add(): lax.all_to_all(outgoing.reshape(dest_count, capacity, block_height, lane_...  9.41 us
    dot_general x1, matrix products, extend_add(): jnp.einsum('qs,sbw->qbw', owner_hits, incoming, precision=lax.Precision.H...  7.83 us
  transfers between devices with their start and end apart: 5, of which 2 were waited for; matrix products, arithmetic and copies ran while one was open for 16% of the time, Pallas kernels for 0%

commit v1 on v0

v1 whole, which is shorter than its diff:
```python
import jax
import jax.numpy as jnp
from jax import lax
from jax.experimental import pallas as pl
from jax.experimental.pallas import tpu as pltpu
from jax.sharding import PartitionSpec as P

BLOCK = 128
MESH = pl.DeviceIdType.MESH
F32 = jnp.float32
BF16 = jnp.bfloat16
STEP, UNSTEP, FRONTS = 13, 5, 32


def parts(front):
    return front // 8, (front // 2) % 4, front % 2


def moved(front, offset, sign):
    (z, y, x), (dz, dy, dx) = parts(front), parts(offset)
    return ((z + sign * dz + 4) % 4) * 8 + ((y + sign * dy + 4) % 4) * 2 + (x + dx) % 2


def slot_of(dest, source):
    (z, y, x), (sz, sy, sx) = parts(dest), parts(source)
    offset = ((z - sz + 4) % 4) * 8 + ((y - sy + 4) % 4) * 2 + (x + sx) % 2
    return (offset * UNSTEP) % FRONTS


def sketch_kernel(
    tab,
    sk_hbm, up_hbm, pi_hbm, lo_hbm, tr_hbm,
    land,
    sk, up, pi, lo, tr, total, uown, usend, urecv, piv, vown, vrecv, solved, keep, pay, precv, summed, sbuf,
    ld, us, ur, vs, vr, ps, pr, ss, sr,
):
    me, row, col = lax.axis_index("front"), lax.axis_index("row"), lax.axis_index("col")
    blocks = total.shape[0]
    mate = {"col": 1 - col}
    twin = {"row": 1 - row}

    def peer(slot):
        offset = (slot * STEP) % FRONTS
        return {"front": moved(me, offset, 1), "col": (col + offset % 2) % 2}

    loads = [
        pltpu.make_async_copy(sk_hbm, sk, ld.at[0]),
        pltpu.make_async_copy(up_hbm, up, ld.at[1]),
        pltpu.make_async_copy(pi_hbm, pi, ld.at[2]),
    ]
    tiles = tr.shape[0]
    for t in range(tiles):
        loads.append(pltpu.make_async_copy(tr_hbm.at[t], tr.at[t], ld.at[3 + t]))
    loads.append(pltpu.make_async_copy(lo_hbm, lo, ld.at[3 + tiles]))
    for copy in loads:
        copy.start()

    barrier = pltpu.get_barrier_semaphore()
    pl.semaphore_signal(barrier, inc=1, device_id=mate, device_id_type=MESH)
    pl.semaphore_signal(barrier, inc=1, device_id=twin, device_id_type=MESH)

    @pl.loop(1, FRONTS)
    def _(slot):
        pl.semaphore_signal(barrier, inc=1, device_id=peer(slot), device_id_type=MESH)

    loads[0].wait()
    height = sk.shape[0]
    bound = tab[0]
    step = 512

    @pl.loop(0, height // step)
    def _(i):
        at = pl.ds(pl.multiple_of(i * step, step), step)
        places = lax.broadcasted_iota(jnp.int32, (step, sk.shape[1]), 0) + (col * height + i * step)
        sk[at, :] = jnp.where(places < bound, sk[at, :].astype(F32), 0.0).astype(BF16)

    half = sk.shape[1] // 2
    loads[1].wait()
    usends = []
    for j in range(2):
        uown[j] = jnp.dot(up[...], sk[:, j * half : (j + 1) * half], preferred_element_type=F32)
        usend[j] = uown[j].astype(BF16)
        if j == 0:
            pl.semaphore_wait(barrier, FRONTS + 1)
        copy = pltpu.make_async_remote_copy(
            src_ref=usend.at[j], dst_ref=urecv.at[j], send_sem=us.at[j], recv_sem=ur.at[j],
            device_id=mate, device_id_type=MESH,
        )
        copy.start()
        usends.append(copy)

    per = blocks // tiles
    for t in range(tiles):
        loads[3 + t].wait()

        part = jnp.dot(tr[t], sk[...], preferred_element_type=F32)
        total[t * per : (t + 1) * per] = part.reshape(per, BLOCK, 2 * half)

    loads[2].wait()
    loads[3 + tiles].wait()
    vsends = []
    for j in range(2):
        usends[j].wait_recv()
        piv[...] = (uown[j] + urecv[j].astype(F32)).astype(BF16)
        vown[j] = jnp.dot(pi[...], piv[...], preferred_element_type=F32)
        copy = pltpu.make_async_remote_copy(
            src_ref=vown.at[j], dst_ref=vrecv.at[j], send_sem=vs.at[j], recv_sem=vr.at[j],
            device_id=twin, device_id_type=MESH,
        )
        copy.start()
        vsends.append(copy)
    for j in range(2):
        vsends[j].wait_recv()
        solved[:, j * half : (j + 1) * half] = (vown[j] + vrecv[j]).astype(BF16)

    def to_mate(p):
        return pltpu.make_async_remote_copy(
            src_ref=pay.at[p], dst_ref=precv.at[p], send_sem=ps.at[p], recv_sem=pr.at[p],
            device_id=mate, device_id_type=MESH,
        )

    def to_owner(slot):
        return pltpu.make_async_remote_copy(
            src_ref=sbuf.at[slot], dst_ref=land.at[slot], send_sem=ss.at[slot], recv_sem=sr.at[slot],
            device_id=peer(slot), device_id_type=MESH,
        )

    @pl.loop(0, blocks)
    def _(p):
        block = tab[1 + p]
        front = total[block] - jnp.dot(lo[block], solved[...], preferred_element_type=F32)
        left, right = front[:, :half], front[:, half:]
        stays = jnp.broadcast_to((tab[1 + blocks + p] + col) % 2, left.shape) == 0
        keep[p] = jnp.where(stays, left, right)
        pay[p] = jnp.where(stays, right, left).astype(BF16)
        to_mate(p).start()

    def fill(slot):
        sbuf[slot] = summed[tab[1 + 2 * blocks + slot]]

    def add(p):
        to_mate(p).wait_recv()
        summed[p] = (keep[p] + precv[p].astype(F32)).astype(BF16)
        fill(p)

    add(0)
    own = pltpu.make_async_copy(sbuf.at[0], land.at[0], ss.at[0])
    own.start()

    @pl.loop(1, blocks)
    def _(p):
        add(p)
        to_owner(p).start()

    @pl.loop(blocks, FRONTS)
    def _(slot):
        fill(slot)
        to_owner(slot).start()

    for j in range(2):
        usends[j].wait_send()
        vsends[j].wait_send()

    @pl.loop(0, blocks)
    def _(p):
        to_mate(p).wait_send()

    own.wait()

    @pl.loop(1, FRONTS)
    def _(slot):
        to_owner(slot).wait()


def sketch_call(tab, sketch, upper, pinv, lower, trailing):
    height, width = sketch.shape
    blocks = lower.shape[0] // BLOCK
    pivot = pinv.shape[0]
    half = width // 2
    tiles = 5
    hbm = pl.BlockSpec(memory_space=pl.ANY)
    return pl.pallas_call(
        sketch_kernel,
        out_shape=jax.ShapeDtypeStruct((FRONTS, BLOCK, half), BF16),
        in_specs=[pl.BlockSpec(memory_space=pltpu.SMEM)] + [hbm] * 5,
        out_specs=hbm,
        scratch_shapes=[
            pltpu.VMEM((height, width), BF16),
            pltpu.VMEM(upper.shape, BF16),
            pltpu.VMEM(pinv.shape, BF16),
            pltpu.VMEM((blocks, BLOCK, pivot), BF16),
            pltpu.VMEM((tiles, trailing.shape[0] // tiles, height), BF16),
            pltpu.VMEM((blocks, BLOCK, width), F32),
            pltpu.VMEM((2, pivot, half), F32),
            pltpu.VMEM((2, pivot, half), BF16),
            pltpu.VMEM((2, pivot, half), BF16),
            pltpu.VMEM((pivot, half), BF16),
            pltpu.VMEM((2, pivot, half), F32),
            pltpu.VMEM((2, pivot, half), F32),
            pltpu.VMEM((pivot, width), BF16),
            pltpu.VMEM((blocks, BLOCK, half), F32),
            pltpu.VMEM((blocks, BLOCK, half), BF16),
            pltpu.VMEM((blocks, BLOCK, half), BF16),
            pltpu.VMEM((blocks, BLOCK, half), BF16),
            pltpu.VMEM((FRONTS, BLOCK, half), BF16),
            pltpu.SemaphoreType.DMA((4 + tiles,)),
            pltpu.SemaphoreType.DMA((2,)),
            pltpu.SemaphoreType.DMA((2,)),
            pltpu.SemaphoreType.DMA((2,)),
            pltpu.SemaphoreType.DMA((2,)),
            pltpu.SemaphoreType.DMA((blocks,)),
            pltpu.SemaphoreType.DMA((blocks,)),
            pltpu.SemaphoreType.DMA((FRONTS,)),
            pltpu.SemaphoreType.DMA((FRONTS,)),
        ],
        compiler_params=pltpu.CompilerParams(
            collective_id=0, has_side_effects=True, vmem_limit_bytes=52 * 2**20
        ),
        cost_estimate=pl.CostEstimate(flops=10_000_000_000, bytes_accessed=100_000_000, transcendentals=0),
        name="sketch",
    )(
        tab, sketch, upper, pinv,
        lower.reshape(blocks, BLOCK, pivot),
        trailing.reshape(tiles, trailing.shape[0] // tiles, height),
    )


def parent_kernel(tags, land, basis, parent, coeff):
    parent[...] = jnp.zeros_like(parent)
    per = parent.shape[0]

    @pl.loop(0, FRONTS)
    def _(slot):
        tag = tags[slot]

        @pl.when(tag < per)
        def _():
            parent[tag] += land[slot].astype(F32)

    rounded = parent[...].astype(BF16).reshape(per * BLOCK, parent.shape[2])
    coeff[...] = lax.dot_general(
        basis[...], rounded, (((0,), (0,)), ((), ())), preferred_element_type=F32
    )


def parent_call(tags, land, basis):
    rows, rank = basis.shape
    half = land.shape[2]
    vmem = pl.BlockSpec(memory_space=pltpu.VMEM)
    return pl.pallas_call(
        parent_kernel,
        out_shape=(
            jax.ShapeDtypeStruct((rows // BLOCK, BLOCK, half), F32),
            jax.ShapeDtypeStruct((rank, half), F32),
        ),
        in_specs=[pl.BlockSpec(memory_space=pltpu.SMEM), vmem, vmem],
        out_specs=(vmem, vmem),
        compiler_params=pltpu.CompilerParams(vmem_limit_bytes=40 * 2**20),
        name="parent",
    )(tags, land, basis)


def residual_kernel(parent, basis, coeff, out):
    out[...] = parent[...] - jnp.dot(basis[...], coeff[...], preferred_element_type=F32)


def residual_call(parent, basis, coeff):
    rows, rank = basis.shape
    half = parent.shape[1]
    tile = 512
    return pl.pallas_call(
        residual_kernel,
        out_shape=jax.ShapeDtypeStruct((rows, half), F32),
        grid=(rows // tile,),
        in_specs=[
            pl.BlockSpec((tile, half), lambda i: (i, 0)),
            pl.BlockSpec((tile, rank), lambda i: (i, 0)),
            pl.BlockSpec((rank, half), lambda i: (0, 0)),
        ],
        out_specs=pl.BlockSpec((tile, half), lambda i: (i, 0)),
        compiler_params=pltpu.CompilerParams(vmem_limit_bytes=40 * 2**20),
        name="residual",
    )(parent, basis, coeff)


def body(bounds, block_map, pivot_inverse, upper_block, lower_block, trailing_block, sketch, basis):
    me, row = lax.axis_index("front"), lax.axis_index("row")
    blocks = block_map.shape[1]
    per = basis.shape[1] // BLOCK
    per_front = per * lax.axis_size("row")
    boundary = bounds[0]
    entries = block_map.reshape(-1)
    order = jnp.arange(blocks, dtype=jnp.int32)
    slots = jnp.arange(FRONTS, dtype=jnp.int32)
    live = (row * blocks + order) * BLOCK < boundary
    everyone = lax.all_gather(jnp.where(live, entries, -1), "front")

    dest = entries // per_front
    slot = jnp.where(live, slot_of(dest, me), FRONTS + order)
    place = jnp.sum((slot[None, :] < slot[:, None]).astype(jnp.int32), axis=1)
    at = (place[None, :] == order[:, None]).astype(jnp.int32)
    block_at = jnp.sum(at * order[None, :], axis=1)
    turned = jnp.sum(at * ((dest + me) % 2)[None, :], axis=1)
    place_of = jnp.sum(jnp.where(slot[None, :] == slots[:, None], place[None, :], 0), axis=1)
    tab = jnp.concatenate([bounds, block_at, turned, place_of])

    land = sketch_call(
        tab, sketch, upper_block[0], pivot_inverse[0], lower_block[0], trailing_block[0]
    )

    mine = (everyone >= 0) & (everyone // per_front == me)
    tag = jnp.sum(jnp.where(mine, everyone % per - per, 0), axis=1) + per
    source = slot_of(me, slots)
    tags = jnp.sum(jnp.where(source[None, :] == slots[:, None], tag[None, :], 0), axis=1)
    parent, part = parent_call(tags, land, basis[0])
    other = lax.ppermute(part, "row", [(0, 1), (1, 0)])
    coefficients = part + other
    residual = residual_call(
        parent.reshape(per * BLOCK, -1), basis[0], coefficients.astype(BF16)
    )
    return coefficients[None], residual[None]


def solution(mesh):
    placed = (
        P("front"),
        P("front", "row"),
        P("front", "col", "row"),
        P("front", "row", "col"),
        P("front", "row", "col"),
        P("front", "row", "col"),
        P("col", None),
        P("front", "row", None),
    )
    return jax.shard_map(
        body,
        mesh=mesh,
        in_specs=placed,
        out_specs=(P("front", None, "col"), P("front", "row", "col")),
        check_vma=False,
    )
```

time: 262 us -> 174 us (0.66)
  waiting for transfers between devices: 108 us -> 1.86 us
  Pallas kernels: 0 us -> 80.6 us
  blocking collectives: 24.3 us -> 82.5 us
  matrix products: 47.7 us -> 0 us
  starting transfers between devices: 38.1 us -> 0.13 us
  local copies, waits for them, and re-layouts: 29.3 us -> 2.64 us
  other arithmetic: 12 us -> 4.32 us
    all_to_all x5 -> x0, waiting for transfers between devices: 108 us -> none  [the longest x1 57.7 us: sum_at_owner(): pieces = lax.all_to_all(split_up(shard, dim, peers), axis, 0, 0, tiled=True)]
    all_gather x0 -> x1, blocking collectives: none -> 82.5 us  [body(): everyone = lax.all_gather(jnp.where(live, entries, -1), 'front')]
    pallas_call x0 -> x3, Pallas kernels: none -> 80.6 us  [the longest x1 74.7 us: sketch_call(): pl.pallas_call(sketch_kernel, out_shape=jax.ShapeDtypeStruct((FRONTS, BLO...]
    dot_general x8 -> x0, matrix products: 47.7 us -> none  [the longest x1 13.2 us: body(): jnp.dot(trailing_block[0], masked, preferred_element_type=jnp.float32)]
    all_to_all x5 -> x0, starting transfers between devices: 38.1 us -> none  [the longest x2 11.7 us: copy_for_each(): lax.all_to_all(jnp.broadcast_to(shard[None], (peers, *shard.shape)), axis...]
    all_to_all x2 -> x0, blocking collectives: 24.3 us -> none  [the longest x1 16.7 us: sum_at_owner(): pieces = lax.all_to_all(split_up(shard, dim, peers), axis, 0, 0, tiled=True)]
    reduce_sum x6 -> x5, other arithmetic: 11.1 us -> 0.65 us  [the longest x1 0.18 us: body(): place = jnp.sum((slot[None, :] < slot[:, None]).astype(jnp.int32), axis=1)]
    dot_general x3 -> x0, local copies, waits for them, and re-layouts: 9.18 us -> none  [the longest x1 4.57 us: extend_add(): jnp.einsum('qs,sbw->qbw', owner_hits, incoming, precision=lax.Precision.H...]
  transfers between devices with their start and end apart: 5 -> 1, of which waited for: 2 -> 1; matrix products, arithmetic and copies ran while one was open for 16% -> 0% of each run, Pallas kernels for 0% -> 0%
where the time goes in v1:
time: 174 us; the launch traced here: 173 us
  blocking collectives  82.5 us (47%)
  Pallas kernels  80.6 us (46%)
  other arithmetic  4.32 us (2%)
  local copies, waits for them, and re-layouts  2.64 us (2%)
  waiting for transfers between devices  1.86 us (1%)
    all_gather x1, blocking collectives, body(): everyone = lax.all_gather(jnp.where(live, entries, -1), 'front')  82.5 us
    pallas_call x1, Pallas kernels, sketch_call(): pl.pallas_call(sketch_kernel, out_shape=jax.ShapeDtypeStruct((FRONTS, BLO...  74.7 us
    pallas_call x1, Pallas kernels, residual_call(): pl.pallas_call(residual_kernel, out_shape=jax.ShapeDtypeStruct((rows, hal...  3.57 us
  transfers between devices with their start and end apart: 1, of which 1 were waited for; matrix products, arithmetic and copies ran while one was open for 0% of the time, Pallas kernels for 0%

profile of v1, /device:TPU:1, one launch (start us, length us, event | category | flops | bytes accessed | tf_op | source)
XLA Modules:
  0.0 173.4 jit_solution(14362423851522585430)
XLA Ops:
  1.3 0.7 compare_select_fusion.32
  2.1 0.7 fusion.31
  2.8 0.2 convert_reduce_fusion
  2.9 0.1 select_reduce_fusion
  3.1 0.1 select_reduce_fusion.3
  3.2 82.5 %all-gather = s32[32,1,20]{2,1,0:T(1,128)S(1)} all-gather(s32[1,1,20]{2,1,0:T(1,128)S(1)} %get-tuple-element.12), channel_id=1, replica_groups=mesh['front'=32,'row'=2,'col'=2] {'front'}, dimensions={0}, use_global_device_ids=true | all-gather | bytes 2640 | tf_op jit(solution)/shard_map/all_gather | solution.py:296
  85.7 1.3 div.108
  87.0 0.1 fusion.3
  87.1 0.1 select_reduce_fusion.1.tags
  87.2 0.1 pad_add_fusion.tab
  87.3 0.0 copy-start.2
  87.3 1.0 copy-done.2
  88.3 0.0 copy-start
  88.3 74.7 %sketch.1.land = bf16[32,128,256]{2,1,0:T(8,128)(2,1)} custom-call(s32[73]{0:T(128)S(1)} %pad_add_fusion.tab, bf16[2560,512]{1,0:T(8,128)(2,1)} %sk_hbm.1, bf16[512,2560]{1,0:T(8,128)(2,1)} %bitcast.58, bf16[512,512]{1,0:T(8,128)(2,1)S(1)} %bitcast.52, bf16[20,128,512]{2,1,0:T(8,128)(2,1)} %bitcast.59, bf16[5,512,2560]{2,1,0:T(8,128)(2,1)} %bitcast.57), custom_call_target="tpu_custom_call" | custom-call | flops 10000000000 | bytes 100000000 | tf_op jit(solution)/shard_map/sketch/pallas_call | solution.py:182
  163.1 0.0 copy-done
  163.1 0.0 copy-start.1
  163.1 1.6 copy-done.1
  164.7 2.3 %parent.1 = (f32[24,128,256]{2,1,0:T(8,128)S(1)}, f32[512,256]{1,0:T(8,128)S(1)}) custom-call(s32[32]{0:T(128)S(1)} %select_reduce_fusion.1.tags, bf16[32,128,256]{2,1,0:T(8,128)(2,1)S(1)} %copy-done.1, bf16[3072,512]{1,0:T(8,128)(2,1)S(1)} %bitcast.49), custom_call_target="tpu_custom_call" | custom-call | tf_op jit(solution)/shard_map/parent/pallas_call | solution.py:250
  167.0 0.1 collective-permute-start
  167.1 1.9 %collective-permute-done = f32[512,256]{1,0:T(8,128)S(1)} collective-permute-done((f32[512,256]{1,0:T(8,128)S(1)}, f32[512,256]{1,0:T(8,128)S(1)}, u32[]{:S(2)}, u32[]{:S(2)}) %collective-permute-start) | collective-permute-done | bytes 524320 | tf_op jit(solution)/shard_map/ppermute | solution.py:316
  169.0 0.9 add_convert_fusion
  169.9 3.6 %residual.1 = f32[3072,256]{1,0:T(8,128)} custom-call(f32[3072,256]{1,0:T(8,128)S(1)} %bitcast.51, bf16[3072,512]{1,0:T(8,128)(2,1)S(1)} %bitcast.50, bf16[512,256]{1,0:T(8,128)(2,1)S(1)} %get-tuple-element.8.coeff), custom_call_target="tpu_custom_call" | custom-call | tf_op jit(solution)/shard_map/residual/pallas_call | solution.py:271
  (3 shorter events, 0.0 us)
Async XLA Ops:
  87.3 1.1 copy-start.2
  88.3 74.8 %copy-start = (bf16[1,3072,512]{2,1,0:T(8,128)(2,1)S(1)}, bf16[1,3072,512]{2,1,0:T(8,128)(2,1)}, u32[]{:S(2)}) copy-start(bf16[1,3072,512]{2,1,0:T(8,128)(2,1)} %param.15) | copy-start | bytes 9437188
  163.1 1.6 copy-start.1
  167.0 2.0 %collective-permute-start = (f32[512,256]{1,0:T(8,128)S(1)}, f32[512,256]{1,0:T(8,128)S(1)}, u32[]{:S(2)}, u32[]{:S(2)}) collective-permute-start(f32[512,256]{1,0:T(8,128)S(1)} %get-tuple-element.4), channel_id=1, source_target_pairs={{0,2},{2,0},{1,3},{3,1},{4,6},{6,4},{5,7},{7,5},{8,10},{10,8},{9,1... | collective-permute-start | bytes 1572872 | tf_op jit(solution)/shard_map/ppermute | solution.py:316

commit v2 on v1

--- a/solution.py
+++ b/solution.py
@@ -28,11 +28,11 @@
 
 
 def sketch_kernel(
-    tab,
+    tab, tile,
     sk_hbm, up_hbm, pi_hbm, lo_hbm, tr_hbm,
-    land,
+    land, marks,
     sk, up, pi, lo, tr, total, uown, usend, urecv, piv, vown, vrecv, solved, keep, pay, precv, summed, sbuf,
-    ld, us, ur, vs, vr, ps, pr, ss, sr,
+    ld, us, ur, vs, vr, ps, pr, ss, sr, ms, mr,
 ):
     me, row, col = lax.axis_index("front"), lax.axis_index("row"), lax.axis_index("col")
     blocks = total.shape[0]
@@ -89,10 +89,22 @@
         copy.start()
         usends.append(copy)
 
+    def mark(slot):
+        return pltpu.make_async_remote_copy(
+            src_ref=tile, dst_ref=marks.at[slot], send_sem=ms.at[slot], recv_sem=mr.at[slot],
+            device_id=peer(slot), device_id_type=MESH,
+        )
+
+    own_mark = pltpu.make_async_copy(tile, marks.at[0], ms.at[0])
+    own_mark.start()
+
+    @pl.loop(1, FRONTS)
+    def _(slot):
+        mark(slot).start()
+
     per = blocks // tiles
     for t in range(tiles):
         loads[3 + t].wait()
-
         part = jnp.dot(tr[t], sk[...], preferred_element_type=F32)
         total[t * per : (t + 1) * per] = part.reshape(per, BLOCK, 2 * half)
 
@@ -166,24 +178,30 @@
         to_mate(p).wait_send()
 
     own.wait()
+    own_mark.wait()
 
     @pl.loop(1, FRONTS)
     def _(slot):
         to_owner(slot).wait()
-
-
-def sketch_call(tab, sketch, upper, pinv, lower, trailing):
+        mark(slot).wait()
+
+
+def sketch_call(tab, tile, sketch, upper, pinv, lower, trailing):
     height, width = sketch.shape
     blocks = lower.shape[0] // BLOCK
     pivot = pinv.shape[0]
     half = width // 2
     tiles = 5
-    hbm = pl.BlockSpec(memory_space=pl.ANY)
+    hbm = pl.BlockSpec(memory_space=pltpu.HBM)
+    vmem = pl.BlockSpec(memory_space=pltpu.VMEM)
     return pl.pallas_call(
         sketch_kernel,
-        out_shape=jax.ShapeDtypeStruct((FRONTS, BLOCK, half), BF16),
-        in_specs=[pl.BlockSpec(memory_space=pltpu.SMEM)] + [hbm] * 5,
-        out_specs=hbm,
+        out_shape=(
+            jax.ShapeDtypeStruct((FRONTS, BLOCK, half), BF16),
+            jax.ShapeDtypeStruct((FRONTS,) + tile.shape, jnp.int32),
+        ),
+        in_specs=[pl.BlockSpec(memory_space=pltpu.SMEM), vmem] + [hbm] * 5,
+        out_specs=(vmem, vmem),
         scratch_shapes=[
             pltpu.VMEM((height, width), BF16),
             pltpu.VMEM(upper.shape, BF16),
@@ -212,14 +230,16 @@
             pltpu.SemaphoreType.DMA((blocks,)),
             pltpu.SemaphoreType.DMA((FRONTS,)),
             pltpu.SemaphoreType.DMA((FRONTS,)),
+            pltpu.SemaphoreType.DMA((FRONTS,)),
+            pltpu.SemaphoreType.DMA((FRONTS,)),
         ],
         compiler_params=pltpu.CompilerParams(
-            collective_id=0, has_side_effects=True, vmem_limit_bytes=52 * 2**20
+            collective_id=0, has_side_effects=True, vmem_limit_bytes=50 * 2**20
         ),
         cost_estimate=pl.CostEstimate(flops=10_000_000_000, bytes_accessed=100_000_000, transcendentals=0),
         name="sketch",
     )(
-        tab, sketch, upper, pinv,
+        tab, tile, sketch, upper, pinv,
         lower.reshape(blocks, BLOCK, pivot),
         trailing.reshape(tiles, trailing.shape[0] // tiles, height),
     )
@@ -260,27 +280,40 @@
     )(tags, land, basis)
 
 
-def residual_kernel(parent, basis, coeff, out):
-    out[...] = parent[...] - jnp.dot(basis[...], coeff[...], preferred_element_type=F32)
-
-
-def residual_call(parent, basis, coeff):
+def residual_kernel(parent, basis, part, other, out, coeff, tile, sems):
+    total = part[...] + other[...]
+    coeff[...] = total
+    rounded = total.astype(BF16)
+    rows = tile.shape[1]
+    copies = []
+    for i in range(parent.shape[0] // rows):
+        if i >= 2:
+            copies[i - 2].wait()
+        at = pl.ds(i * rows, rows)
+        tile[i % 2] = parent[at, :] - jnp.dot(basis[at, :], rounded, preferred_element_type=F32)
+        copy = pltpu.make_async_copy(tile.at[i % 2], out.at[at, :], sems.at[i % 2])
+        copy.start()
+        copies.append(copy)
+    copies[-2].wait()
+    copies[-1].wait()
+
+
+def residual_call(parent, basis, part, other):
     rows, rank = basis.shape
     half = parent.shape[1]
-    tile = 512
+    vmem = pl.BlockSpec(memory_space=pltpu.VMEM)
     return pl.pallas_call(
         residual_kernel,
-        out_shape=jax.ShapeDtypeStruct((rows, half), F32),
-        grid=(rows // tile,),
-        in_specs=[
-            pl.BlockSpec((tile, half), lambda i: (i, 0)),
-            pl.BlockSpec((tile, rank), lambda i: (i, 0)),
-            pl.BlockSpec((rank, half), lambda i: (0, 0)),
-        ],
-        out_specs=pl.BlockSpec((tile, half), lambda i: (i, 0)),
+        out_shape=(
+            jax.ShapeDtypeStruct((rows, half), F32),
+            jax.ShapeDtypeStruct((rank, half), F32),
+        ),
+        in_specs=[vmem] * 4,
+        out_specs=(pl.BlockSpec(memory_space=pltpu.HBM), vmem),
+        scratch_shapes=[pltpu.VMEM((2, 512, half), F32), pltpu.SemaphoreType.DMA((2,))],
         compiler_params=pltpu.CompilerParams(vmem_limit_bytes=40 * 2**20),
         name="residual",
-    )(parent, basis, coeff)
+    )(parent, basis, part, other)
 
 
 def body(bounds, block_map, pivot_inverse, upper_block, lower_block, trailing_block, sketch, basis):
@@ -293,7 +326,6 @@
     order = jnp.arange(blocks, dtype=jnp.int32)
     slots = jnp.arange(FRONTS, dtype=jnp.int32)
     live = (row * blocks + order) * BLOCK < boundary
-    everyone = lax.all_gather(jnp.where(live, entries, -1), "front")
 
     dest = entries // per_front
     slot = jnp.where(live, slot_of(dest, me), FRONTS + order)
@@ -303,20 +335,21 @@
     turned = jnp.sum(at * ((dest + me) % 2)[None, :], axis=1)
     place_of = jnp.sum(jnp.where(slot[None, :] == slots[:, None], place[None, :], 0), axis=1)
     tab = jnp.concatenate([bounds, block_at, turned, place_of])
-
-    land = sketch_call(
-        tab, sketch, upper_block[0], pivot_inverse[0], lower_block[0], trailing_block[0]
-    )
-
-    mine = (everyone >= 0) & (everyone // per_front == me)
-    tag = jnp.sum(jnp.where(mine, everyone % per - per, 0), axis=1) + per
-    source = slot_of(me, slots)
-    tags = jnp.sum(jnp.where(source[None, :] == slots[:, None], tag[None, :], 0), axis=1)
+    tag = jnp.sum(
+        jnp.where(slot[None, :] == slots[:, None], (entries % per - per)[None, :], 0), axis=1
+    ) + per
+    tile = jnp.broadcast_to(jnp.pad(tag, (0, 128 - FRONTS))[None, :], (8, 128))
+
+    land, marks = sketch_call(
+        tab, tile, sketch, upper_block[0], pivot_inverse[0], lower_block[0], trailing_block[0]
+    )
+    tags = jnp.sum(
+        jnp.where(jnp.arange(128, dtype=jnp.int32)[None, :] == slots[:, None], marks[:, 0, :], 0), axis=1
+    )
     parent, part = parent_call(tags, land, basis[0])
     other = lax.ppermute(part, "row", [(0, 1), (1, 0)])
-    coefficients = part + other
-    residual = residual_call(
-        parent.reshape(per * BLOCK, -1), basis[0], coefficients.astype(BF16)
+    residual, coefficients = residual_call(
+        parent.reshape(per * BLOCK, -1), basis[0], part, other
     )
     return coefficients[None], residual[None]
 

time: 174 us -> 86.3 us (0.50)
  blocking collectives: 82.5 us -> 0 us
  other arithmetic: 4.32 us -> 2 us
    all_gather x1 -> x0, blocking collectives: 82.5 us -> none  [body(): everyone = lax.all_gather(jnp.where(live, entries, -1), 'front')]
where the time goes in v2:
time: 86.3 us; the launch traced here: 86.1 us
  Pallas kernels  79.2 us (92%)
  other arithmetic  2 us (2%)
  waiting for transfers between devices  1.54 us (2%)
  between operations  1.38 us (2%)
  local copies, waits for them, and re-layouts  1.06 us (1%)
  starting transfers between devices  0.93 us (1%)
    pallas_call x1, Pallas kernels, sketch_call(): pl.pallas_call(sketch_kernel, out_shape=(jax.ShapeDtypeStruct((FRONTS, BL...  71.9 us
    pallas_call x1, Pallas kernels, residual_call(): pl.pallas_call(residual_kernel, out_shape=(jax.ShapeDtypeStruct((rows, ha...  4.9 us
    pallas_call x1, Pallas kernels, parent_call(): pl.pallas_call(parent_kernel, out_shape=(jax.ShapeDtypeStruct((rows // BL...  2.4 us
  transfers between devices with their start and end apart: 1, of which 1 were waited for; matrix products, arithmetic and copies ran while one was open for 0% of the time, Pallas kernels for 0%

profile of v2, /device:TPU:1, one launch (start us, length us, event | category | flops | bytes accessed | tf_op | source)
XLA Modules:
  0.0 86.1 jit_solution(12120086871154286361)
XLA Ops:
  1.3 0.7 compare_select_fusion.22
  2.0 0.7 fusion.14
  2.7 0.2 convert_reduce_fusion
  2.9 0.1 select_reduce_fusion.4
  3.0 0.1 select_reduce_fusion.1
  3.2 0.1 pad_add_fusion.tab
  3.2 0.0 copy-start.1
  3.2 1.0 %copy-done.1 = bf16[1,512,512]{2,1,0:T(8,128)(2,1)S(1)} copy-done((bf16[1,512,512]{2,1,0:T(8,128)(2,1)S(1)}, bf16[1,512,512]{2,1,0:T(8,128)(2,1)}, u32[]{:S(2)}) %copy-start.1) | copy-done | bytes 524312
  4.3 0.0 copy-start
  4.3 71.9 %sketch.1 = (bf16[32,128,256]{2,1,0:T(8,128)(2,1)S(1)}, s32[32,8,128]{2,1,0:T(8,128)S(1)}) custom-call(s32[73]{0:T(128)S(1)} %pad_add_fusion.tab, s32[8,128]{1,0:T(8,128)S(1)} %broadcast_in_dim.54.tile, bf16[2560,512]{1,0:T(8,128)(2,1)} %sk_hbm.1, bf16[512,2560]{1,0:T(8,128)(2,1)} %bitcast.33, bf16[512,512]{1,0:T(8,128)(2,1)S(1)} %bitcast.29, ...), custom_call_target="tpu_custom_call" | custom-call | flops 10000000000 | bytes 100000000 | tf_op jit(solution)/shard_map/sketch/pallas_call | solution.py:197
  76.2 0.1 select_reduce_fusion.tags
  76.3 0.0 copy-done
  76.3 2.4 %parent.1 = (f32[24,128,256]{2,1,0:T(8,128)S(1)}, f32[512,256]{1,0:T(8,128)S(1)}) custom-call(s32[32]{0:T(128)S(1)} %select_reduce_fusion.tags, bf16[32,128,256]{2,1,0:T(8,128)(2,1)S(1)} %get-tuple-element.9.land, bf16[3072,512]{1,0:T(8,128)(2,1)S(1)} %bitcast.26), custom_call_target="tpu_custom_call" | custom-call | tf_op jit(solution)/shard_map/parent/pallas_call | solution.py:270
  78.7 0.9 %collective-permute-start = (f32[512,256]{1,0:T(8,128)S(1)}, f32[512,256]{1,0:T(8,128)S(1)}, u32[]{:S(2)}, u32[]{:S(2)}) collective-permute-start(f32[512,256]{1,0:T(8,128)S(1)} %get-tuple-element.11.part), channel_id=1, source_target_pairs={{0,2},{2,0},{1,3},{3,1},{4,6},{6,4},{5,7},{7,5},{8,10},{10,8},{9,1... | collective-permute-start | bytes 1572872 | tf_op jit(solution)/shard_map/ppermute | solution.py:350
  79.7 1.5 %collective-permute-done.other = f32[512,256]{1,0:T(8,128)S(1)} collective-permute-done((f32[512,256]{1,0:T(8,128)S(1)}, f32[512,256]{1,0:T(8,128)S(1)}, u32[]{:S(2)}, u32[]{:S(2)}) %collective-permute-start) | collective-permute-done | bytes 524320 | tf_op jit(solution)/shard_map/ppermute | solution.py:350
  81.2 4.9 %residual.1 = (f32[3072,256]{1,0:T(8,128)}, f32[512,256]{1,0:T(8,128)}) custom-call(f32[3072,256]{1,0:T(8,128)S(1)} %bitcast.28, bf16[3072,512]{1,0:T(8,128)(2,1)S(1)} %bitcast.27, f32[512,256]{1,0:T(8,128)S(1)} %get-tuple-element.11.part, f32[512,256]{1,0:T(8,128)S(1)} %collective-permute-done.other), custom_call_target="tpu_custom_call" | custom-call | tf_op jit(solution)/shard_map/residual/pallas_call | solution.py:305
  (4 shorter events, 0.0 us)
Async XLA Ops:
  3.2 1.0 %copy-start.1 = (bf16[1,512,512]{2,1,0:T(8,128)(2,1)S(1)}, bf16[1,512,512]{2,1,0:T(8,128)(2,1)}, u32[]{:S(2)}) copy-start(bf16[1,512,512]{2,1,0:T(8,128)(2,1)} %param.10) | copy-start | bytes 1572868
  4.3 72.0 %copy-start = (bf16[1,3072,512]{2,1,0:T(8,128)(2,1)S(1)}, bf16[1,3072,512]{2,1,0:T(8,128)(2,1)}, u32[]{:S(2)}) copy-start(bf16[1,3072,512]{2,1,0:T(8,128)(2,1)} %param.15) | copy-start | bytes 9437188
  78.7 2.5 %collective-permute-start = (f32[512,256]{1,0:T(8,128)S(1)}, f32[512,256]{1,0:T(8,128)S(1)}, u32[]{:S(2)}, u32[]{:S(2)}) collective-permute-start(f32[512,256]{1,0:T(8,128)S(1)} %get-tuple-element.11.part), channel_id=1, source_target_pairs={{0,2},{2,0},{1,3},{3,1},{4,6},{6,4},{5,7},{7,5},{8,10},{10,8},{9,1... | collective-permute-start | bytes 1572872 | tf_op jit(solution)/shard_map/ppermute | solution.py:350

commit v3 on v2

--- a/solution.py
+++ b/solution.py
@@ -9,22 +9,22 @@
 MESH = pl.DeviceIdType.MESH
 F32 = jnp.float32
 BF16 = jnp.bfloat16
-STEP, UNSTEP, FRONTS = 13, 5, 32
-
-
-def parts(front):
-    return front // 8, (front // 2) % 4, front % 2
-
-
-def moved(front, offset, sign):
-    (z, y, x), (dz, dy, dx) = parts(front), parts(offset)
-    return ((z + sign * dz + 4) % 4) * 8 + ((y + sign * dy + 4) % 4) * 2 + (x + dx) % 2
+FRONTS = 32
+ORDER = (
+    (2, 2, 1), (2, 2, 0), (2, 1, 1), (1, 2, 1), (2, 3, 0), (2, 3, 1), (3, 2, 1), (1, 2, 0), (1, 1, 1), (3, 3, 1),
+    (2, 1, 0), (1, 3, 1), (3, 1, 1), (3, 2, 0), (0, 2, 1), (2, 0, 1), (0, 2, 0), (0, 3, 1), (1, 0, 1), (2, 0, 0),
+    (3, 0, 1), (1, 1, 0), (3, 3, 0), (0, 1, 1), (1, 3, 0), (3, 1, 0), (0, 0, 1), (0, 1, 0), (1, 0, 0), (0, 3, 0),
+    (3, 0, 0), (0, 0, 0),
+)
+HERE = FRONTS - 1
 
 
 def slot_of(dest, source):
-    (z, y, x), (sz, sy, sx) = parts(dest), parts(source)
-    offset = ((z - sz + 4) % 4) * 8 + ((y - sy + 4) % 4) * 2 + (x + sx) % 2
-    return (offset * UNSTEP) % FRONTS
+    (z, y, x), (sz, sy, sx) = ((f >> 3, (f >> 1) & 3, f & 1) for f in (dest, source))
+    offset = (((z - sz) & 3) << 3) + (((y - sy) & 3) << 1) + (x ^ sx)
+    codes = jnp.asarray([dz * 8 + dy * 2 + dx for dz, dy, dx in ORDER], jnp.int32)
+    slots = jnp.arange(FRONTS, dtype=jnp.int32)
+    return jnp.sum(jnp.where(offset[:, None] == codes[None, :], slots[None, :], 0), axis=1)
 
 
 def sketch_kernel(
@@ -39,9 +39,16 @@
     mate = {"col": 1 - col}
     twin = {"row": 1 - row}
 
+    depth, width = me // 8, (me // 2) % 4
+    depths = [((depth + d) % 4) * 8 for d in range(4)]
+    widths = [((width + d) % 4) * 2 for d in range(4)]
+    near = [me % 2, 1 - me % 2]
+    cols = [col, 1 - col]
+    others = [slot for slot in range(FRONTS) if slot != HERE]
+
     def peer(slot):
-        offset = (slot * STEP) % FRONTS
-        return {"front": moved(me, offset, 1), "col": (col + offset % 2) % 2}
+        dz, dy, dx = ORDER[slot]
+        return {"front": depths[dz] + widths[dy] + near[dx], "col": cols[dx]}
 
     loads = [
         pltpu.make_async_copy(sk_hbm, sk, ld.at[0]),
@@ -59,8 +66,7 @@
     pl.semaphore_signal(barrier, inc=1, device_id=mate, device_id_type=MESH)
     pl.semaphore_signal(barrier, inc=1, device_id=twin, device_id_type=MESH)
 
-    @pl.loop(1, FRONTS)
-    def _(slot):
+    for slot in others:
         pl.semaphore_signal(barrier, inc=1, device_id=peer(slot), device_id_type=MESH)
 
     loads[0].wait()
@@ -95,11 +101,9 @@
             device_id=peer(slot), device_id_type=MESH,
         )
 
-    own_mark = pltpu.make_async_copy(tile, marks.at[0], ms.at[0])
+    own_mark = pltpu.make_async_copy(tile, marks.at[HERE], ms.at[HERE])
     own_mark.start()
-
-    @pl.loop(1, FRONTS)
-    def _(slot):
+    for slot in others:
         mark(slot).start()
 
     per = blocks // tiles
@@ -155,19 +159,16 @@
         summed[p] = (keep[p] + precv[p].astype(F32)).astype(BF16)
         fill(p)
 
-    add(0)
-    own = pltpu.make_async_copy(sbuf.at[0], land.at[0], ss.at[0])
-    own.start()
-
-    @pl.loop(1, blocks)
-    def _(p):
-        add(p)
-        to_owner(p).start()
-
-    @pl.loop(blocks, FRONTS)
-    def _(slot):
-        fill(slot)
-        to_owner(slot).start()
+    own = pltpu.make_async_copy(sbuf.at[HERE], land.at[HERE], ss.at[HERE])
+    for slot in range(FRONTS):
+        if slot < blocks:
+            add(slot)
+        else:
+            fill(slot)
+        if slot == HERE:
+            own.start()
+        else:
+            to_owner(slot).start()
 
     for j in range(2):
         usends[j].wait_send()
@@ -180,8 +181,7 @@
     own.wait()
     own_mark.wait()
 
-    @pl.loop(1, FRONTS)
-    def _(slot):
+    for slot in others:
         to_owner(slot).wait()
         mark(slot).wait()
 

time: 86.3 us -> 80 us (0.927)
  Pallas kernels: 79.2 us -> 72.5 us
    pallas_call x1, Pallas kernels: 71.9 us -> 65.2 us  [sketch_call(): pl.pallas_call(sketch_kernel, out_shape=(jax.ShapeDtypeStruct((FRONTS, BL...]
where the time goes in v3:
time: 80 us; the launch traced here: 79.8 us
  Pallas kernels  72.5 us (91%)
  other arithmetic  2.79 us (3%)
  waiting for transfers between devices  1.54 us (2%)
  between operations  1.35 us (2%)
  local copies, waits for them, and re-layouts  1.06 us (1%)
    pallas_call x1, Pallas kernels, sketch_call(): pl.pallas_call(sketch_kernel, out_shape=(jax.ShapeDtypeStruct((FRONTS, BL...  65.2 us
    pallas_call x1, Pallas kernels, residual_call(): pl.pallas_call(residual_kernel, out_shape=(jax.ShapeDtypeStruct((rows, ha...  4.9 us
    pallas_call x1, Pallas kernels, parent_call(): pl.pallas_call(parent_kernel, out_shape=(jax.ShapeDtypeStruct((rows // BL...  2.39 us
  transfers between devices with their start and end apart: 1, of which 1 were waited for; matrix products, arithmetic and copies ran while one was open for 0% of the time, Pallas kernels for 0%

profile of v3, /device:TPU:1, one launch (start us, length us, event | category | flops | bytes accessed | tf_op | source)
XLA Modules:
  0.0 79.8 jit_solution(1393983028095363394)
XLA Ops:
  1.3 0.7 fusion.1
  2.0 0.7 xor_add_fusion
  2.6 0.8 %select_reduce_fusion.5 = s32[20]{0:T(128)S(1)} fusion(s32[32]{0:T(128)} %constant.62.clone, s32[20]{0:T(128)S(1)} %xor_add_fusion), kind=kLoop, calls=%fused_computation.9 | loop fusion | flops 1900 | bytes 288 | tf_op jit(solution)/shard_map/reduce_sum | solution.py:27
  3.5 0.2 convert_reduce_fusion
  3.7 0.1 select_reduce_fusion.4
  3.8 0.1 select_reduce_fusion.1
  3.9 0.1 pad_add_fusion.tab
  4.0 0.0 copy-start.1
  4.0 1.0 %copy-done.1 = bf16[1,512,512]{2,1,0:T(8,128)(2,1)S(1)} copy-done((bf16[1,512,512]{2,1,0:T(8,128)(2,1)S(1)}, bf16[1,512,512]{2,1,0:T(8,128)(2,1)}, u32[]{:S(2)}) %copy-start.1) | copy-done | bytes 524312
  5.0 0.0 copy-start
  5.0 65.2 %sketch.1 = (bf16[32,128,256]{2,1,0:T(8,128)(2,1)S(1)}, s32[32,8,128]{2,1,0:T(8,128)S(1)}) custom-call(s32[73]{0:T(128)S(1)} %pad_add_fusion.tab, s32[8,128]{1,0:T(8,128)S(1)} %broadcast_in_dim.71.tile, bf16[2560,512]{1,0:T(8,128)(2,1)} %sk_hbm.1, bf16[512,2560]{1,0:T(8,128)(2,1)} %bitcast.30, bf16[512,512]{1,0:T(8,128)(2,1)S(1)} %bitcast.26, ...), custom_call_target="tpu_custom_call" | custom-call | flops 10000000000 | bytes 100000000 | tf_op jit(solution)/shard_map/sketch/pallas_call | solution.py:197
  70.3 0.1 select_reduce_fusion.tags
  70.4 0.0 copy-done
  70.4 2.4 %parent.1 = (f32[24,128,256]{2,1,0:T(8,128)S(1)}, f32[512,256]{1,0:T(8,128)S(1)}) custom-call(s32[32]{0:T(128)S(1)} %select_reduce_fusion.tags, bf16[32,128,256]{2,1,0:T(8,128)(2,1)S(1)} %get-tuple-element.9.land, bf16[3072,512]{1,0:T(8,128)(2,1)S(1)} %bitcast.23), custom_call_target="tpu_custom_call" | custom-call | tf_op jit(solution)/shard_map/parent/pallas_call | solution.py:270
  72.8 0.6 collective-permute-start
  73.4 1.5 %collective-permute-done.other = f32[512,256]{1,0:T(8,128)S(1)} collective-permute-done((f32[512,256]{1,0:T(8,128)S(1)}, f32[512,256]{1,0:T(8,128)S(1)}, u32[]{:S(2)}, u32[]{:S(2)}) %collective-permute-start) | collective-permute-done | bytes 524320 | tf_op jit(solution)/shard_map/ppermute | solution.py:350
  74.9 4.9 %residual.1 = (f32[3072,256]{1,0:T(8,128)}, f32[512,256]{1,0:T(8,128)}) custom-call(f32[3072,256]{1,0:T(8,128)S(1)} %bitcast.25, bf16[3072,512]{1,0:T(8,128)(2,1)S(1)} %bitcast.24, f32[512,256]{1,0:T(8,128)S(1)} %get-tuple-element.11.part, f32[512,256]{1,0:T(8,128)S(1)} %collective-permute-done.other), custom_call_target="tpu_custom_call" | custom-call | tf_op jit(solution)/shard_map/residual/pallas_call | solution.py:305
  (5 shorter events, 0.0 us)
Async XLA Ops:
  4.0 1.0 %copy-start.1 = (bf16[1,512,512]{2,1,0:T(8,128)(2,1)S(1)}, bf16[1,512,512]{2,1,0:T(8,128)(2,1)}, u32[]{:S(2)}) copy-start(bf16[1,512,512]{2,1,0:T(8,128)(2,1)} %param.11) | copy-start | bytes 1572868
  5.0 65.3 %copy-start = (bf16[1,3072,512]{2,1,0:T(8,128)(2,1)S(1)}, bf16[1,3072,512]{2,1,0:T(8,128)(2,1)}, u32[]{:S(2)}) copy-start(bf16[1,3072,512]{2,1,0:T(8,128)(2,1)} %param.16) | copy-start | bytes 9437188
  72.8 2.1 %collective-permute-start = (f32[512,256]{1,0:T(8,128)S(1)}, f32[512,256]{1,0:T(8,128)S(1)}, u32[]{:S(2)}, u32[]{:S(2)}) collective-permute-start(f32[512,256]{1,0:T(8,128)S(1)} %get-tuple-element.11.part), channel_id=1, source_target_pairs={{0,2},{2,0},{1,3},{3,1},{4,6},{6,4},{5,7},{7,5},{8,10},{10,8},{9,1... | collective-permute-start | bytes 1572872 | tf_op jit(solution)/shard_map/ppermute | solution.py:350

commit v4 on v3

--- a/solution.py
+++ b/solution.py
@@ -17,6 +17,7 @@
     (3, 0, 0), (0, 0, 0),
 )
 HERE = FRONTS - 1
+EARLY = 4
 
 
 def slot_of(dest, source):
@@ -51,14 +52,22 @@
         return {"front": depths[dz] + widths[dy] + near[dx], "col": cols[dx]}
 
     loads = [
-        pltpu.make_async_copy(sk_hbm, sk, ld.at[0]),
-        pltpu.make_async_copy(up_hbm, up, ld.at[1]),
-        pltpu.make_async_copy(pi_hbm, pi, ld.at[2]),
+        pltpu.make_async_copy(up_hbm, up, ld.at[0]),
+        pltpu.make_async_copy(pi_hbm, pi, ld.at[1]),
     ]
+    quarter = sk.shape[1] // 4
     tiles = tr.shape[0]
+    columns = [
+        pltpu.make_async_copy(
+            sk_hbm.at[:, pl.ds(q * quarter, quarter)], sk.at[:, pl.ds(i * quarter, quarter)], ld.at[3 + tiles + i]
+        )
+        for i, q in enumerate((0, 2, 1, 3))
+    ]
+    for copy in columns:
+        copy.start()
     for t in range(tiles):
-        loads.append(pltpu.make_async_copy(tr_hbm.at[t], tr.at[t], ld.at[3 + t]))
-    loads.append(pltpu.make_async_copy(lo_hbm, lo, ld.at[3 + tiles]))
+        loads.append(pltpu.make_async_copy(tr_hbm.at[t], tr.at[t], ld.at[2 + t]))
+    loads.append(pltpu.make_async_copy(lo_hbm, lo, ld.at[2 + tiles]))
     for copy in loads:
         copy.start()
 
@@ -69,7 +78,8 @@
     for slot in others:
         pl.semaphore_signal(barrier, inc=1, device_id=peer(slot), device_id_type=MESH)
 
-    loads[0].wait()
+    for copy in columns:
+        copy.wait()
     height = sk.shape[0]
     bound = tab[0]
     step = 512
@@ -81,19 +91,22 @@
         sk[at, :] = jnp.where(places < bound, sk[at, :].astype(F32), 0.0).astype(BF16)
 
     half = sk.shape[1] // 2
-    loads[1].wait()
+    loads[0].wait()
     usends = []
+    depth = up.shape[0] // 2
     for j in range(2):
-        uown[j] = jnp.dot(up[...], sk[:, j * half : (j + 1) * half], preferred_element_type=F32)
-        usend[j] = uown[j].astype(BF16)
-        if j == 0:
-            pl.semaphore_wait(barrier, FRONTS + 1)
-        copy = pltpu.make_async_remote_copy(
-            src_ref=usend.at[j], dst_ref=urecv.at[j], send_sem=us.at[j], recv_sem=ur.at[j],
-            device_id=mate, device_id_type=MESH,
-        )
-        copy.start()
-        usends.append(copy)
+        for h in range(2):
+            at = pl.ds(h * depth, depth)
+            uown[j, at, :] = jnp.dot(up[at, :], sk[:, j * half : (j + 1) * half], preferred_element_type=F32)
+            usend[j, at, :] = uown[j, at, :].astype(BF16)
+            if not usends:
+                pl.semaphore_wait(barrier, FRONTS + 1)
+            copy = pltpu.make_async_remote_copy(
+                src_ref=usend.at[j, at], dst_ref=urecv.at[j, at], send_sem=us.at[2 * j + h], recv_sem=ur.at[2 * j + h],
+                device_id=mate, device_id_type=MESH,
+            )
+            copy.start()
+            usends.append(copy)
 
     def mark(slot):
         return pltpu.make_async_remote_copy(
@@ -108,15 +121,39 @@
 
     per = blocks // tiles
     for t in range(tiles):
-        loads[3 + t].wait()
+        loads[2 + t].wait()
         part = jnp.dot(tr[t], sk[...], preferred_element_type=F32)
         total[t * per : (t + 1) * per] = part.reshape(per, BLOCK, 2 * half)
 
-    loads[2].wait()
-    loads[3 + tiles].wait()
+    loads[1].wait()
+    loads[2 + tiles].wait()
+
+    def part_of(p, t):
+        return pltpu.make_async_remote_copy(
+            src_ref=pay.at[p, t], dst_ref=precv.at[p, t], send_sem=ps.at[p, t], recv_sem=pr.at[p, t],
+            device_id=mate, device_id_type=MESH,
+        )
+
+    def to_mate(p):
+        return pltpu.make_async_remote_copy(
+            src_ref=pay.at[p], dst_ref=precv.at[p], send_sem=ps.at[p, 0], recv_sem=pr.at[p, 0],
+            device_id=mate, device_id_type=MESH,
+        )
+
+    def put(p, front, t):
+        left, right = front[:, :quarter], front[:, quarter:]
+        stays = jnp.broadcast_to((tab[1 + blocks + p] + col) % 2, left.shape) == 0
+        keep[p, :, t * quarter : (t + 1) * quarter] = jnp.where(stays, left, right)
+        pay[p, t] = jnp.where(stays, right, left).astype(BF16)
+
+    def half_front(p, t):
+        block = tab[1 + p]
+        at = slice(t * half, (t + 1) * half)
+        return total[block, :, at] - jnp.dot(lo[block], solved[:, at], preferred_element_type=F32)
+
     vsends = []
-    for j in range(2):
-        usends[j].wait_recv()
+
+    def solve(j):
         piv[...] = (uown[j] + urecv[j].astype(F32)).astype(BF16)
         vown[j] = jnp.dot(pi[...], piv[...], preferred_element_type=F32)
         copy = pltpu.make_async_remote_copy(
@@ -125,15 +162,34 @@
         )
         copy.start()
         vsends.append(copy)
-    for j in range(2):
+
+    def settle(j):
         vsends[j].wait_recv()
         solved[:, j * half : (j + 1) * half] = (vown[j] + vrecv[j]).astype(BF16)
 
-    def to_mate(p):
-        return pltpu.make_async_remote_copy(
-            src_ref=pay.at[p], dst_ref=precv.at[p], send_sem=ps.at[p], recv_sem=pr.at[p],
-            device_id=mate, device_id_type=MESH,
-        )
+    usends[0].wait_recv()
+    usends[1].wait_recv()
+    solve(0)
+    settle(0)
+    for p in range(EARLY):
+        put(p, half_front(p, 0), 0)
+    usends[2].wait_recv()
+    usends[3].wait_recv()
+    for p in range(EARLY):
+        part_of(p, 0).start()
+    solve(1)
+    settle(1)
+    for p in range(EARLY):
+        put(p, half_front(p, 1), 1)
+        part_of(p, 1).start()
+
+    @pl.loop(EARLY, blocks)
+    def _(p):
+        block = tab[1 + p]
+        front = total[block] - jnp.dot(lo[block], solved[...], preferred_element_type=F32)
+        put(p, front[:, :half], 0)
+        put(p, front[:, half:], 1)
+        to_mate(p).start()
 
     def to_owner(slot):
         return pltpu.make_async_remote_copy(
@@ -141,22 +197,18 @@
             device_id=peer(slot), device_id_type=MESH,
         )
 
-    @pl.loop(0, blocks)
-    def _(p):
-        block = tab[1 + p]
-        front = total[block] - jnp.dot(lo[block], solved[...], preferred_element_type=F32)
-        left, right = front[:, :half], front[:, half:]
-        stays = jnp.broadcast_to((tab[1 + blocks + p] + col) % 2, left.shape) == 0
-        keep[p] = jnp.where(stays, left, right)
-        pay[p] = jnp.where(stays, right, left).astype(BF16)
-        to_mate(p).start()
-
     def fill(slot):
         sbuf[slot] = summed[tab[1 + 2 * blocks + slot]]
 
     def add(p):
-        to_mate(p).wait_recv()
-        summed[p] = (keep[p] + precv[p].astype(F32)).astype(BF16)
+        if p < EARLY:
+            part_of(p, 0).wait_recv()
+            part_of(p, 1).wait_recv()
+        else:
+            to_mate(p).wait_recv()
+        for t in range(2):
+            at = slice(t * quarter, (t + 1) * quarter)
+            summed[p, :, at] = (keep[p, :, at] + precv[p, t].astype(F32)).astype(BF16)
         fill(p)
 
     own = pltpu.make_async_copy(sbuf.at[HERE], land.at[HERE], ss.at[HERE])
@@ -170,11 +222,13 @@
         else:
             to_owner(slot).start()
 
-    for j in range(2):
-        usends[j].wait_send()
-        vsends[j].wait_send()
-
-    @pl.loop(0, blocks)
+    for copy in usends + vsends:
+        copy.wait_send()
+    for p in range(EARLY):
+        part_of(p, 0).wait_send()
+        part_of(p, 1).wait_send()
+
+    @pl.loop(EARLY, blocks)
     def _(p):
         to_mate(p).wait_send()
 
@@ -217,17 +271,17 @@
             pltpu.VMEM((2, pivot, half), F32),
             pltpu.VMEM((pivot, width), BF16),
             pltpu.VMEM((blocks, BLOCK, half), F32),
-            pltpu.VMEM((blocks, BLOCK, half), BF16),
-            pltpu.VMEM((blocks, BLOCK, half), BF16),
+            pltpu.VMEM((blocks, 2, BLOCK, half // 2), BF16),
+            pltpu.VMEM((blocks, 2, BLOCK, half // 2), BF16),
             pltpu.VMEM((blocks, BLOCK, half), BF16),
             pltpu.VMEM((FRONTS, BLOCK, half), BF16),
-            pltpu.SemaphoreType.DMA((4 + tiles,)),
+            pltpu.SemaphoreType.DMA((8 + tiles,)),
+            pltpu.SemaphoreType.DMA((4,)),
+            pltpu.SemaphoreType.DMA((4,)),
             pltpu.SemaphoreType.DMA((2,)),
             pltpu.SemaphoreType.DMA((2,)),
-            pltpu.SemaphoreType.DMA((2,)),
-            pltpu.SemaphoreType.DMA((2,)),
-            pltpu.SemaphoreType.DMA((blocks,)),
-            pltpu.SemaphoreType.DMA((blocks,)),
+            pltpu.SemaphoreType.DMA((blocks, 2)),
+            pltpu.SemaphoreType.DMA((blocks, 2)),
             pltpu.SemaphoreType.DMA((FRONTS,)),
             pltpu.SemaphoreType.DMA((FRONTS,)),
             pltpu.SemaphoreType.DMA((FRONTS,)),
@@ -286,16 +340,14 @@
     rounded = total.astype(BF16)
     rows = tile.shape[1]
     copies = []
-    for i in range(parent.shape[0] // rows):
-        if i >= 2:
-            copies[i - 2].wait()
+    for i in range(tile.shape[0]):
         at = pl.ds(i * rows, rows)
-        tile[i % 2] = parent[at, :] - jnp.dot(basis[at, :], rounded, preferred_element_type=F32)
-        copy = pltpu.make_async_copy(tile.at[i % 2], out.at[at, :], sems.at[i % 2])
+        tile[i] = parent[at, :] - jnp.dot(basis[at, :], rounded, preferred_element_type=F32)
+        copy = pltpu.make_async_copy(tile.at[i], out.at[at, :], sems.at[i])
         copy.start()
         copies.append(copy)
-    copies[-2].wait()
-    copies[-1].wait()
+    for copy in copies:
+        copy.wait()
 
 
 def residual_call(parent, basis, part, other):
@@ -310,8 +362,8 @@
         ),
         in_specs=[vmem] * 4,
         out_specs=(pl.BlockSpec(memory_space=pltpu.HBM), vmem),
-        scratch_shapes=[pltpu.VMEM((2, 512, half), F32), pltpu.SemaphoreType.DMA((2,))],
-        compiler_params=pltpu.CompilerParams(vmem_limit_bytes=40 * 2**20),
+        scratch_shapes=[pltpu.VMEM((rows // 512, 512, half), F32), pltpu.SemaphoreType.DMA((rows // 512,))],
+        compiler_params=pltpu.CompilerParams(vmem_limit_bytes=24 * 2**20),
         name="residual",
     )(parent, basis, part, other)
 

time: 80 us -> 76.5 us (0.956)
  Pallas kernels: 72.5 us -> 68.6 us
    pallas_call x1, Pallas kernels: 65.2 us -> 63.2 us  [sketch_call(): pl.pallas_call(sketch_kernel, out_shape=(jax.ShapeDtypeStruct((FRONTS, BL...]
    pallas_call x1, Pallas kernels: 4.9 us -> 3 us  [residual_call(): pl.pallas_call(residual_kernel, out_shape=(jax.ShapeDtypeStruct((rows, ha...]
where the time goes in v4:
time: 76.5 us; the launch traced here: 76.3 us
  Pallas kernels  68.6 us (90%)
  other arithmetic  2.79 us (4%)
  waiting for transfers between devices  1.54 us (2%)
  between operations  1.35 us (2%)
  local copies, waits for them, and re-layouts  1.06 us (1%)
  starting transfers between devices  0.94 us (1%)
    pallas_call x1, Pallas kernels, sketch_call(): pl.pallas_call(sketch_kernel, out_shape=(jax.ShapeDtypeStruct((FRONTS, BL...  63.2 us
    pallas_call x1, Pallas kernels, residual_call(): pl.pallas_call(residual_kernel, out_shape=(jax.ShapeDtypeStruct((rows, ha...  3 us
    pallas_call x1, Pallas kernels, parent_call(): pl.pallas_call(parent_kernel, out_shape=(jax.ShapeDtypeStruct((rows // BL...  2.38 us
    ppermute x1, waiting for transfers between devices, body(): other = lax.ppermute(part, 'row', [(0, 1), (1, 0)])  1.54 us
  transfers between devices with their start and end apart: 1, of which 1 were waited for; matrix products, arithmetic and copies ran while one was open for 0% of the time, Pallas kernels for 0%

profile of v4, /device:TPU:1, one launch (start us, length us, event | category | flops | bytes accessed | tf_op | source)
XLA Modules:
  0.0 76.3 jit_solution(174540994676355909)
XLA Ops:
  1.3 0.7 fusion.1
  2.0 0.7 xor_add_fusion
  2.6 0.8 %select_reduce_fusion.5 = s32[20]{0:T(128)S(1)} fusion(s32[32]{0:T(128)} %constant.62.clone, s32[20]{0:T(128)S(1)} %xor_add_fusion), kind=kLoop, calls=%fused_computation.9 | loop fusion | flops 1900 | bytes 288 | tf_op jit(solution)/shard_map/reduce_sum | solution.py:28
  3.5 0.2 convert_reduce_fusion
  3.7 0.1 select_reduce_fusion.4
  3.8 0.1 select_reduce_fusion.1
  3.9 0.1 pad_add_fusion.tab
  4.0 0.0 copy-start.1
  4.0 1.0 %copy-done.1 = bf16[1,512,512]{2,1,0:T(8,128)(2,1)S(1)} copy-done((bf16[1,512,512]{2,1,0:T(8,128)(2,1)S(1)}, bf16[1,512,512]{2,1,0:T(8,128)(2,1)}, u32[]{:S(2)}) %copy-start.1) | copy-done | bytes 524312
  5.0 0.0 copy-start
  5.0 63.2 %sketch.1 = (bf16[32,128,256]{2,1,0:T(8,128)(2,1)S(1)}, s32[32,8,128]{2,1,0:T(8,128)S(1)}) custom-call(s32[73]{0:T(128)S(1)} %pad_add_fusion.tab, s32[8,128]{1,0:T(8,128)S(1)} %broadcast_in_dim.71.tile, bf16[2560,512]{1,0:T(8,128)(2,1)} %sk_hbm.1, bf16[512,2560]{1,0:T(8,128)(2,1)} %bitcast.30, bf16[512,512]{1,0:T(8,128)(2,1)S(1)} %bitcast.26, ...), custom_call_target="tpu_custom_call" | custom-call | flops 10000000000 | bytes 100000000 | tf_op jit(solution)/shard_map/sketch/pallas_call | solution.py:251
  68.3 0.1 select_reduce_fusion.tags
  68.4 0.0 copy-done
  68.4 2.4 %parent.1 = (f32[24,128,256]{2,1,0:T(8,128)S(1)}, f32[512,256]{1,0:T(8,128)S(1)}) custom-call(s32[32]{0:T(128)S(1)} %select_reduce_fusion.tags, bf16[32,128,256]{2,1,0:T(8,128)(2,1)S(1)} %get-tuple-element.9.land, bf16[3072,512]{1,0:T(8,128)(2,1)S(1)} %bitcast.23), custom_call_target="tpu_custom_call" | custom-call | tf_op jit(solution)/shard_map/parent/pallas_call | solution.py:324
  70.8 0.9 %collective-permute-start = (f32[512,256]{1,0:T(8,128)S(1)}, f32[512,256]{1,0:T(8,128)S(1)}, u32[]{:S(2)}, u32[]{:S(2)}) collective-permute-start(f32[512,256]{1,0:T(8,128)S(1)} %get-tuple-element.11.part), channel_id=1, source_target_pairs={{0,2},{2,0},{1,3},{3,1},{4,6},{6,4},{5,7},{7,5},{8,10},{10,8},{9,1... | collective-permute-start | bytes 1572872 | tf_op jit(solution)/shard_map/ppermute | solution.py:402
  71.8 1.5 %collective-permute-done.other = f32[512,256]{1,0:T(8,128)S(1)} collective-permute-done((f32[512,256]{1,0:T(8,128)S(1)}, f32[512,256]{1,0:T(8,128)S(1)}, u32[]{:S(2)}, u32[]{:S(2)}) %collective-permute-start) | collective-permute-done | bytes 524320 | tf_op jit(solution)/shard_map/ppermute | solution.py:402
  73.3 3.0 %residual.1 = (f32[3072,256]{1,0:T(8,128)}, f32[512,256]{1,0:T(8,128)}) custom-call(f32[3072,256]{1,0:T(8,128)S(1)} %bitcast.25, bf16[3072,512]{1,0:T(8,128)(2,1)S(1)} %bitcast.24, f32[512,256]{1,0:T(8,128)S(1)} %get-tuple-element.11.part, f32[512,256]{1,0:T(8,128)S(1)} %collective-permute-done.other), custom_call_target="tpu_custom_call" | custom-call | tf_op jit(solution)/shard_map/residual/pallas_call | solution.py:357
  (5 shorter events, 0.0 us)
Async XLA Ops:
  4.0 1.0 %copy-start.1 = (bf16[1,512,512]{2,1,0:T(8,128)(2,1)S(1)}, bf16[1,512,512]{2,1,0:T(8,128)(2,1)}, u32[]{:S(2)}) copy-start(bf16[1,512,512]{2,1,0:T(8,128)(2,1)} %param.11) | copy-start | bytes 1572868
  5.0 63.4 %copy-start = (bf16[1,3072,512]{2,1,0:T(8,128)(2,1)S(1)}, bf16[1,3072,512]{2,1,0:T(8,128)(2,1)}, u32[]{:S(2)}) copy-start(bf16[1,3072,512]{2,1,0:T(8,128)(2,1)} %param.16) | copy-start | bytes 9437188
  70.8 2.5 %collective-permute-start = (f32[512,256]{1,0:T(8,128)S(1)}, f32[512,256]{1,0:T(8,128)S(1)}, u32[]{:S(2)}, u32[]{:S(2)}) collective-permute-start(f32[512,256]{1,0:T(8,128)S(1)} %get-tuple-element.11.part), channel_id=1, source_target_pairs={{0,2},{2,0},{1,3},{3,1},{4,6},{6,4},{5,7},{7,5},{8,10},{10,8},{9,1... | collective-permute-start | bytes 1572872 | tf_op jit(solution)/shard_map/ppermute | solution.py:402

commit v5 on v4

--- a/solution.py
+++ b/solution.py
@@ -1,3 +1,5 @@
+import functools
+
 import jax
 import jax.numpy as jnp
 from jax import lax
@@ -20,20 +22,47 @@
 EARLY = 4
 
 
-def slot_of(dest, source):
-    (z, y, x), (sz, sy, sx) = ((f >> 3, (f >> 1) & 3, f & 1) for f in (dest, source))
-    offset = (((z - sz) & 3) << 3) + (((y - sy) & 3) << 1) + (x ^ sx)
-    codes = jnp.asarray([dz * 8 + dy * 2 + dx for dz, dy, dx in ORDER], jnp.int32)
-    slots = jnp.arange(FRONTS, dtype=jnp.int32)
-    return jnp.sum(jnp.where(offset[:, None] == codes[None, :], slots[None, :], 0), axis=1)
+def total_over(values, axis):
+    return jnp.sum(values, axis=axis, keepdims=True)
+
+
+def tables_of(entries, bound, me, row, per):
+    blocks = entries.shape[1]
+    down = lax.broadcasted_iota(jnp.int32, (blocks, blocks), 0)
+    along = lax.broadcasted_iota(jnp.int32, (blocks, blocks), 1)
+    order = lax.broadcasted_iota(jnp.int32, (blocks, 1), 0)
+    slots = lax.broadcasted_iota(jnp.int32, (blocks, FRONTS), 1)
+    held = total_over(jnp.where(down == along, jnp.broadcast_to(entries, (blocks, blocks)), 0), 1)
+    dest = total_over((held >= 2 * per * (slots + 1)).astype(jnp.int32), 1)
+    depth, width, near = dest >> 3, (dest >> 1) & 3, dest & 1
+    turned = (near + me % 2) & 1
+    offset = (((depth - me // 8) & 3) << 3) + (((width - (me // 2) % 4) & 3) << 1) + turned
+    slot = jnp.zeros_like(offset)
+    for s, (dz, dy, dx) in enumerate(ORDER):
+        slot = jnp.where(offset == dz * 8 + dy * 2 + dx, s, slot)
+    slot = jnp.where((row * blocks + order) * BLOCK < bound, slot, FRONTS + order)
+    wide = jnp.broadcast_to(slot, (blocks, blocks))
+    slot_along = total_over(jnp.where(down == along, wide, 0), 0)
+    place = total_over((slot_along < wide).astype(jnp.int32), 1)
+    at = place == along
+    hit = slot == slots
+    rest = held - 2 * per * dest
+    local = jnp.where(rest >= per, rest - per, rest)
+    return (
+        total_over(jnp.where(at, down, 0), 0),
+        total_over(jnp.where(at, turned, 0), 0),
+        total_over(jnp.where(hit, place, 0), 0),
+        total_over(jnp.where(hit, local - per, 0), 0) + per,
+    )
 
 
 def sketch_kernel(
-    tab, tile,
+    per_device,
+    bounds, block_map,
     sk_hbm, up_hbm, pi_hbm, lo_hbm, tr_hbm,
     land, marks,
-    sk, up, pi, lo, tr, total, uown, usend, urecv, piv, vown, vrecv, solved, keep, pay, precv, summed, sbuf,
-    ld, us, ur, vs, vr, ps, pr, ss, sr, ms, mr,
+    tile, tabv, tab, sk, up, pi, lo, tr, total, uown, usend, urecv, piv, vown, vrecv, solved, keep, pay, precv, summed, sbuf,
+    ld, us, ur, vs, vr, ps, pr, ss, sr, ms, mr, ts,
 ):
     me, row, col = lax.axis_index("front"), lax.axis_index("row"), lax.axis_index("col")
     blocks = total.shape[0]
@@ -81,7 +110,7 @@
     for copy in columns:
         copy.wait()
     height = sk.shape[0]
-    bound = tab[0]
+    bound = bounds[0]
     step = 512
 
     @pl.loop(0, height // step)
@@ -114,6 +143,14 @@
             device_id=peer(slot), device_id_type=MESH,
         )
 
+    rows_of = tables_of(block_map[...], bound, me, row, per_device)
+    tile[...] = jnp.zeros_like(tile)
+    tile[:, :FRONTS] = jnp.broadcast_to(rows_of[3], (tile.shape[0], FRONTS))
+    tabv[...] = jnp.zeros_like(tabv)
+    for i in range(3):
+        tabv[i : i + 1, : rows_of[i].shape[1]] = rows_of[i]
+    to_scalars = pltpu.make_async_copy(tabv, tab, ts)
+    to_scalars.start()
     own_mark = pltpu.make_async_copy(tile, marks.at[HERE], ms.at[HERE])
     own_mark.start()
     for slot in others:
@@ -125,6 +162,7 @@
         part = jnp.dot(tr[t], sk[...], preferred_element_type=F32)
         total[t * per : (t + 1) * per] = part.reshape(per, BLOCK, 2 * half)
 
+    to_scalars.wait()
     loads[1].wait()
     loads[2 + tiles].wait()
 
@@ -142,12 +180,12 @@
 
     def put(p, front, t):
         left, right = front[:, :quarter], front[:, quarter:]
-        stays = jnp.broadcast_to((tab[1 + blocks + p] + col) % 2, left.shape) == 0
+        stays = jnp.broadcast_to((tab[1, p] + col) % 2, left.shape) == 0
         keep[p, :, t * quarter : (t + 1) * quarter] = jnp.where(stays, left, right)
         pay[p, t] = jnp.where(stays, right, left).astype(BF16)
 
     def half_front(p, t):
-        block = tab[1 + p]
+        block = tab[0, p]
         at = slice(t * half, (t + 1) * half)
         return total[block, :, at] - jnp.dot(lo[block], solved[:, at], preferred_element_type=F32)
 
@@ -185,7 +223,7 @@
 
     @pl.loop(EARLY, blocks)
     def _(p):
-        block = tab[1 + p]
+        block = tab[0, p]
         front = total[block] - jnp.dot(lo[block], solved[...], preferred_element_type=F32)
         put(p, front[:, :half], 0)
         put(p, front[:, half:], 1)
@@ -198,7 +236,7 @@
         )
 
     def fill(slot):
-        sbuf[slot] = summed[tab[1 + 2 * blocks + slot]]
+        sbuf[slot] = summed[tab[2, slot]]
 
     def add(p):
         if p < EARLY:
@@ -240,7 +278,7 @@
         mark(slot).wait()
 
 
-def sketch_call(tab, tile, sketch, upper, pinv, lower, trailing):
+def sketch_call(per_device, bounds, block_map, sketch, upper, pinv, lower, trailing):
     height, width = sketch.shape
     blocks = lower.shape[0] // BLOCK
     pivot = pinv.shape[0]
@@ -249,14 +287,17 @@
     hbm = pl.BlockSpec(memory_space=pltpu.HBM)
     vmem = pl.BlockSpec(memory_space=pltpu.VMEM)
     return pl.pallas_call(
-        sketch_kernel,
+        functools.partial(sketch_kernel, per_device),
         out_shape=(
             jax.ShapeDtypeStruct((FRONTS, BLOCK, half), BF16),
-            jax.ShapeDtypeStruct((FRONTS,) + tile.shape, jnp.int32),
+            jax.ShapeDtypeStruct((FRONTS, 8, 128), jnp.int32),
         ),
         in_specs=[pl.BlockSpec(memory_space=pltpu.SMEM), vmem] + [hbm] * 5,
         out_specs=(vmem, vmem),
         scratch_shapes=[
+            pltpu.VMEM((8, 128), jnp.int32),
+            pltpu.VMEM((8, 128), jnp.int32),
+            pltpu.SMEM((8, 128), jnp.int32),
             pltpu.VMEM((height, width), BF16),
             pltpu.VMEM(upper.shape, BF16),
             pltpu.VMEM(pinv.shape, BF16),
@@ -286,6 +327,7 @@
             pltpu.SemaphoreType.DMA((FRONTS,)),
             pltpu.SemaphoreType.DMA((FRONTS,)),
             pltpu.SemaphoreType.DMA((FRONTS,)),
+            pltpu.SemaphoreType.DMA,
         ],
         compiler_params=pltpu.CompilerParams(
             collective_id=0, has_side_effects=True, vmem_limit_bytes=50 * 2**20
@@ -293,7 +335,7 @@
         cost_estimate=pl.CostEstimate(flops=10_000_000_000, bytes_accessed=100_000_000, transcendentals=0),
         name="sketch",
     )(
-        tab, tile, sketch, upper, pinv,
+        bounds, block_map, sketch, upper, pinv,
         lower.reshape(blocks, BLOCK, pivot),
         trailing.reshape(tiles, trailing.shape[0] // tiles, height),
     )
@@ -369,31 +411,10 @@
 
 
 def body(bounds, block_map, pivot_inverse, upper_block, lower_block, trailing_block, sketch, basis):
-    me, row = lax.axis_index("front"), lax.axis_index("row")
-    blocks = block_map.shape[1]
     per = basis.shape[1] // BLOCK
-    per_front = per * lax.axis_size("row")
-    boundary = bounds[0]
-    entries = block_map.reshape(-1)
-    order = jnp.arange(blocks, dtype=jnp.int32)
     slots = jnp.arange(FRONTS, dtype=jnp.int32)
-    live = (row * blocks + order) * BLOCK < boundary
-
-    dest = entries // per_front
-    slot = jnp.where(live, slot_of(dest, me), FRONTS + order)
-    place = jnp.sum((slot[None, :] < slot[:, None]).astype(jnp.int32), axis=1)
-    at = (place[None, :] == order[:, None]).astype(jnp.int32)
-    block_at = jnp.sum(at * order[None, :], axis=1)
-    turned = jnp.sum(at * ((dest + me) % 2)[None, :], axis=1)
-    place_of = jnp.sum(jnp.where(slot[None, :] == slots[:, None], place[None, :], 0), axis=1)
-    tab = jnp.concatenate([bounds, block_at, turned, place_of])
-    tag = jnp.sum(
-        jnp.where(slot[None, :] == slots[:, None], (entries % per - per)[None, :], 0), axis=1
-    ) + per
-    tile = jnp.broadcast_to(jnp.pad(tag, (0, 128 - FRONTS))[None, :], (8, 128))
-
     land, marks = sketch_call(
-        tab, tile, sketch, upper_block[0], pivot_inverse[0], lower_block[0], trailing_block[0]
+        per, bounds, block_map, sketch, upper_block[0], pivot_inverse[0], lower_block[0], trailing_block[0]
     )
     tags = jnp.sum(
         jnp.where(jnp.arange(128, dtype=jnp.int32)[None, :] == slots[:, None], marks[:, 0, :], 0), axis=1

time: 76.5 us -> 74.1 us (0.969)
  other arithmetic: 2.79 us -> 0.11 us
    reduce_sum x4 -> x0, other arithmetic: 1.23 us -> none  [the longest x1 0.84 us: slot_of(): jnp.sum(jnp.where(offset[:, None] == codes[None, :], slots[None, :], 0),...]
    unnamed x4 -> x6, local copies, waits for them, and re-layouts: 1.05 us -> 1.69 us
where the time goes in v5:
time: 74.1 us; the launch traced here: 73.9 us
  Pallas kernels  68.5 us (92%)
  local copies, waits for them, and re-layouts  1.7 us (2%)
  waiting for transfers between devices  1.54 us (2%)
  between operations  1.32 us (2%)
    pallas_call x1, Pallas kernels, sketch_call(): pl.pallas_call(functools.partial(sketch_kernel, per_device), out_shape=(j...  63.2 us
    pallas_call x1, Pallas kernels, residual_call(): pl.pallas_call(residual_kernel, out_shape=(jax.ShapeDtypeStruct((rows, ha...  2.96 us
    pallas_call x1, Pallas kernels, parent_call(): pl.pallas_call(parent_kernel, out_shape=(jax.ShapeDtypeStruct((rows // BL...  2.4 us
    unnamed x6, local copies, waits for them, and re-layouts  1.69 us
    ppermute x1, waiting for transfers between devices, body(): other = lax.ppermute(part, 'row', [(0, 1), (1, 0)])  1.54 us
  transfers between devices with their start and end apart: 1, of which 1 were waited for; matrix products, arithmetic and copies ran while one was open for 0% of the time, Pallas kernels for 0%

profile of v5, /device:TPU:1, one launch (start us, length us, event | category | flops | bytes accessed | tf_op | source)
XLA Modules:
  0.0 73.9 jit_solution(4228933060867210384)
XLA Ops:
  1.3 0.0 copy-start.1
  1.3 1.0 %copy-done.1 = bf16[1,512,512]{2,1,0:T(8,128)(2,1)S(1)} copy-done((bf16[1,512,512]{2,1,0:T(8,128)(2,1)S(1)}, bf16[1,512,512]{2,1,0:T(8,128)(2,1)}, u32[]{:S(2)}) %copy-start.1) | copy-done | bytes 524312
  2.3 0.0 copy-start.2
  2.3 0.7 copy-done.2
  3.0 0.0 copy-start
  3.0 63.2 %sketch.1 = (bf16[32,128,256]{2,1,0:T(8,128)(2,1)S(1)}, s32[32,8,128]{2,1,0:T(8,128)S(1)}) custom-call(s32[1]{0:T(128)S(6)} %copy.10.bounds, s32[1,20]{1,0:T(1,128)S(1)} %copy-done.2, bf16[2560,512]{1,0:T(8,128)(2,1)} %sk_hbm.1, bf16[512,2560]{1,0:T(8,128)(2,1)} %bitcast.16, bf16[512,512]{1,0:T(8,128)(2,1)S(1)} %bitcast.12, bf16[20,128,512]{2,1,0:T(8,128)(2,1)} %bitcast.17, ...), custom_call_target="tpu_custom_call" | custom-call | flops 10000000000 | bytes 100000000 | tf_op jit(solution)/shard_map/sketch/pallas_call | solution.py:289
  66.2 0.1 select_reduce_fusion.tags
  66.3 0.0 copy-done
  66.3 2.4 %parent.1 = (f32[24,128,256]{2,1,0:T(8,128)S(1)}, f32[512,256]{1,0:T(8,128)S(1)}) custom-call(s32[32]{0:T(128)S(1)} %select_reduce_fusion.tags, bf16[32,128,256]{2,1,0:T(8,128)(2,1)S(1)} %get-tuple-element.9.land, bf16[3072,512]{1,0:T(8,128)(2,1)S(1)} %bitcast.9), custom_call_target="tpu_custom_call" | custom-call | tf_op jit(solution)/shard_map/parent/pallas_call | solution.py:366
  68.7 0.7 collective-permute-start
  69.4 1.5 %collective-permute-done.other = f32[512,256]{1,0:T(8,128)S(1)} collective-permute-done((f32[512,256]{1,0:T(8,128)S(1)}, f32[512,256]{1,0:T(8,128)S(1)}, u32[]{:S(2)}, u32[]{:S(2)}) %collective-permute-start) | collective-permute-done | bytes 524320 | tf_op jit(solution)/shard_map/ppermute | solution.py:423
  70.9 3.0 %residual.1 = (f32[3072,256]{1,0:T(8,128)}, f32[512,256]{1,0:T(8,128)}) custom-call(f32[3072,256]{1,0:T(8,128)S(1)} %bitcast.11, bf16[3072,512]{1,0:T(8,128)(2,1)S(1)} %bitcast.10, f32[512,256]{1,0:T(8,128)S(1)} %get-tuple-element.11.part, f32[512,256]{1,0:T(8,128)S(1)} %collective-permute-done.other), custom_call_target="tpu_custom_call" | custom-call | tf_op jit(solution)/shard_map/residual/pallas_call | solution.py:399
  (1 shorter events, 0.0 us)
Async XLA Ops:
  1.3 1.0 %copy-start.1 = (bf16[1,512,512]{2,1,0:T(8,128)(2,1)S(1)}, bf16[1,512,512]{2,1,0:T(8,128)(2,1)}, u32[]{:S(2)}) copy-start(bf16[1,512,512]{2,1,0:T(8,128)(2,1)} %param.10) | copy-start | bytes 1572868
  2.3 0.7 copy-start.2
  3.0 63.3 %copy-start = (bf16[1,3072,512]{2,1,0:T(8,128)(2,1)S(1)}, bf16[1,3072,512]{2,1,0:T(8,128)(2,1)}, u32[]{:S(2)}) copy-start(bf16[1,3072,512]{2,1,0:T(8,128)(2,1)} %param.15) | copy-start | bytes 9437188
  68.7 2.2 %collective-permute-start = (f32[512,256]{1,0:T(8,128)S(1)}, f32[512,256]{1,0:T(8,128)S(1)}, u32[]{:S(2)}, u32[]{:S(2)}) collective-permute-start(f32[512,256]{1,0:T(8,128)S(1)} %get-tuple-element.11.part), channel_id=1, source_target_pairs={{0,2},{2,0},{1,3},{3,1},{4,6},{6,4},{5,7},{7,5},{8,10},{10,8},{9,1... | collective-permute-start | bytes 1572872 | tf_op jit(solution)/shard_map/ppermute | solution.py:423

commit v6 on v5

--- a/solution.py
+++ b/solution.py
@@ -211,10 +211,9 @@
     settle(0)
     for p in range(EARLY):
         put(p, half_front(p, 0), 0)
+        part_of(p, 0).start()
     usends[2].wait_recv()
     usends[3].wait_recv()
-    for p in range(EARLY):
-        part_of(p, 0).start()
     solve(1)
     settle(1)
     for p in range(EARLY):
@@ -376,10 +375,11 @@
     )(tags, land, basis)
 
 
-def residual_kernel(parent, basis, part, other, out, coeff, tile, sems):
-    total = part[...] + other[...]
-    coeff[...] = total
-    rounded = total.astype(BF16)
+def residual_kernel(parent, basis, part, other, out, coeff, tile, total, sems):
+    total[...] = part[...] + other[...]
+    whole = pltpu.make_async_copy(total, coeff, sems.at[tile.shape[0]])
+    whole.start()
+    rounded = total[...].astype(BF16)
     rows = tile.shape[1]
     copies = []
     for i in range(tile.shape[0]):
@@ -388,6 +388,7 @@
         copy = pltpu.make_async_copy(tile.at[i], out.at[at, :], sems.at[i])
         copy.start()
         copies.append(copy)
+    whole.wait()
     for copy in copies:
         copy.wait()
 
@@ -395,7 +396,9 @@
 def residual_call(parent, basis, part, other):
     rows, rank = basis.shape
     half = parent.shape[1]
+    tile = 256
     vmem = pl.BlockSpec(memory_space=pltpu.VMEM)
+    hbm = pl.BlockSpec(memory_space=pltpu.HBM)
     return pl.pallas_call(
         residual_kernel,
         out_shape=(
@@ -403,8 +406,12 @@
             jax.ShapeDtypeStruct((rank, half), F32),
         ),
         in_specs=[vmem] * 4,
-        out_specs=(pl.BlockSpec(memory_space=pltpu.HBM), vmem),
-        scratch_shapes=[pltpu.VMEM((rows // 512, 512, half), F32), pltpu.SemaphoreType.DMA((rows // 512,))],
+        out_specs=(hbm, hbm),
+        scratch_shapes=[
+            pltpu.VMEM((rows // tile, tile, half), F32),
+            pltpu.VMEM((rank, half), F32),
+            pltpu.SemaphoreType.DMA((rows // tile + 1,)),
+        ],
         compiler_params=pltpu.CompilerParams(vmem_limit_bytes=24 * 2**20),
         name="residual",
     )(parent, basis, part, other)

time: 74.1 us -> 72.5 us (0.978)
  Pallas kernels: 68.5 us -> 67 us
    pallas_call x1, Pallas kernels: 2.96 us -> 2.1 us  [residual_call(): pl.pallas_call(residual_kernel, out_shape=(jax.ShapeDtypeStruct((rows, ha...]
where the time goes in v6:
time: 72.5 us; the launch traced here: 72.4 us
  Pallas kernels  67 us (92%)
  local copies, waits for them, and re-layouts  1.7 us (2%)
  waiting for transfers between devices  1.54 us (2%)
  between operations  1.32 us (2%)
    pallas_call x1, Pallas kernels, sketch_call(): pl.pallas_call(functools.partial(sketch_kernel, per_device), out_shape=(j...  62.6 us
    pallas_call x1, Pallas kernels, parent_call(): pl.pallas_call(parent_kernel, out_shape=(jax.ShapeDtypeStruct((rows // BL...  2.31 us
    pallas_call x1, Pallas kernels, residual_call(): pl.pallas_call(residual_kernel, out_shape=(jax.ShapeDtypeStruct((rows, ha...  2.1 us
    unnamed x6, local copies, waits for them, and re-layouts  1.69 us
    ppermute x1, waiting for transfers between devices, body(): other = lax.ppermute(part, 'row', [(0, 1), (1, 0)])  1.54 us
  transfers between devices with their start and end apart: 1, of which 1 were waited for; matrix products, arithmetic and copies ran while one was open for 0% of the time, Pallas kernels for 0%

profile of v6, /device:TPU:1, one launch (start us, length us, event | category | flops | bytes accessed | tf_op | source)
XLA Modules:
  0.0 72.4 jit_solution(8017414488175600785)
XLA Ops:
  1.3 0.0 copy-start.1
  1.3 1.0 %copy-done.1 = bf16[1,512,512]{2,1,0:T(8,128)(2,1)S(1)} copy-done((bf16[1,512,512]{2,1,0:T(8,128)(2,1)S(1)}, bf16[1,512,512]{2,1,0:T(8,128)(2,1)}, u32[]{:S(2)}) %copy-start.1) | copy-done | bytes 524312
  2.3 0.0 copy-start.2
  2.3 0.7 copy-done.2
  3.0 0.0 copy-start
  3.0 62.6 %sketch.1 = (bf16[32,128,256]{2,1,0:T(8,128)(2,1)S(1)}, s32[32,8,128]{2,1,0:T(8,128)S(1)}) custom-call(s32[1]{0:T(128)S(6)} %copy.10.bounds, s32[1,20]{1,0:T(1,128)S(1)} %copy-done.2, bf16[2560,512]{1,0:T(8,128)(2,1)} %sk_hbm.1, bf16[512,2560]{1,0:T(8,128)(2,1)} %bitcast.16, bf16[512,512]{1,0:T(8,128)(2,1)S(1)} %bitcast.12, bf16[20,128,512]{2,1,0:T(8,128)(2,1)} %bitcast.17, ...), custom_call_target="tpu_custom_call" | custom-call | flops 10000000000 | bytes 100000000 | tf_op jit(solution)/shard_map/sketch/pallas_call | solution.py:288
  65.6 0.1 select_reduce_fusion.tags
  65.7 0.0 copy-done
  65.7 2.3 %parent.1 = (f32[24,128,256]{2,1,0:T(8,128)S(1)}, f32[512,256]{1,0:T(8,128)S(1)}) custom-call(s32[32]{0:T(128)S(1)} %select_reduce_fusion.tags, bf16[32,128,256]{2,1,0:T(8,128)(2,1)S(1)} %get-tuple-element.9.land, bf16[3072,512]{1,0:T(8,128)(2,1)S(1)} %bitcast.9), custom_call_target="tpu_custom_call" | custom-call | tf_op jit(solution)/shard_map/parent/pallas_call | solution.py:365
  68.0 0.7 collective-permute-start
  68.7 1.5 %collective-permute-done.other = f32[512,256]{1,0:T(8,128)S(1)} collective-permute-done((f32[512,256]{1,0:T(8,128)S(1)}, f32[512,256]{1,0:T(8,128)S(1)}, u32[]{:S(2)}, u32[]{:S(2)}) %collective-permute-start) | collective-permute-done | bytes 524320 | tf_op jit(solution)/shard_map/ppermute | solution.py:430
  70.3 2.1 %residual.1 = (f32[3072,256]{1,0:T(8,128)}, f32[512,256]{1,0:T(8,128)}) custom-call(f32[3072,256]{1,0:T(8,128)S(1)} %bitcast.11, bf16[3072,512]{1,0:T(8,128)(2,1)S(1)} %bitcast.10, f32[512,256]{1,0:T(8,128)S(1)} %get-tuple-element.11.part, f32[512,256]{1,0:T(8,128)S(1)} %collective-permute-done.other), custom_call_target="tpu_custom_call" | custom-call | tf_op jit(solution)/shard_map/residual/pallas_call | solution.py:402
  (1 shorter events, 0.0 us)
Async XLA Ops:
  1.3 1.0 %copy-start.1 = (bf16[1,512,512]{2,1,0:T(8,128)(2,1)S(1)}, bf16[1,512,512]{2,1,0:T(8,128)(2,1)}, u32[]{:S(2)}) copy-start(bf16[1,512,512]{2,1,0:T(8,128)(2,1)} %param.10) | copy-start | bytes 1572868
  2.3 0.7 copy-start.2
  3.0 62.7 %copy-start = (bf16[1,3072,512]{2,1,0:T(8,128)(2,1)S(1)}, bf16[1,3072,512]{2,1,0:T(8,128)(2,1)}, u32[]{:S(2)}) copy-start(bf16[1,3072,512]{2,1,0:T(8,128)(2,1)} %param.15) | copy-start | bytes 9437188
  68.0 2.3 %collective-permute-start = (f32[512,256]{1,0:T(8,128)S(1)}, f32[512,256]{1,0:T(8,128)S(1)}, u32[]{:S(2)}, u32[]{:S(2)}) collective-permute-start(f32[512,256]{1,0:T(8,128)S(1)} %get-tuple-element.11.part), channel_id=1, source_target_pairs={{0,2},{2,0},{1,3},{3,1},{4,6},{6,4},{5,7},{7,5},{8,10},{10,8},{9,1... | collective-permute-start | bytes 1572872 | tf_op jit(solution)/shard_map/ppermute | solution.py:430

commit v7 on v6

--- a/solution.py
+++ b/solution.py
@@ -19,7 +19,6 @@
     (3, 0, 0), (0, 0, 0),
 )
 HERE = FRONTS - 1
-EARLY = 4
 
 
 def total_over(values, axis):
@@ -172,16 +171,10 @@
             device_id=mate, device_id_type=MESH,
         )
 
-    def to_mate(p):
-        return pltpu.make_async_remote_copy(
-            src_ref=pay.at[p], dst_ref=precv.at[p], send_sem=ps.at[p, 0], recv_sem=pr.at[p, 0],
-            device_id=mate, device_id_type=MESH,
-        )
-
     def put(p, front, t):
         left, right = front[:, :quarter], front[:, quarter:]
         stays = jnp.broadcast_to((tab[1, p] + col) % 2, left.shape) == 0
-        keep[p, :, t * quarter : (t + 1) * quarter] = jnp.where(stays, left, right)
+        keep[p, t] = jnp.where(stays, left, right)
         pay[p, t] = jnp.where(stays, right, left).astype(BF16)
 
     def half_front(p, t):
@@ -205,75 +198,49 @@
         vsends[j].wait_recv()
         solved[:, j * half : (j + 1) * half] = (vown[j] + vrecv[j]).astype(BF16)
 
-    usends[0].wait_recv()
-    usends[1].wait_recv()
-    solve(0)
-    settle(0)
-    for p in range(EARLY):
-        put(p, half_front(p, 0), 0)
-        part_of(p, 0).start()
-    usends[2].wait_recv()
-    usends[3].wait_recv()
-    solve(1)
-    settle(1)
-    for p in range(EARLY):
-        put(p, half_front(p, 1), 1)
-        part_of(p, 1).start()
-
-    @pl.loop(EARLY, blocks)
-    def _(p):
-        block = tab[0, p]
-        front = total[block] - jnp.dot(lo[block], solved[...], preferred_element_type=F32)
-        put(p, front[:, :half], 0)
-        put(p, front[:, half:], 1)
-        to_mate(p).start()
-
-    def to_owner(slot):
+    for j in range(2):
+        usends[2 * j].wait_recv()
+        usends[2 * j + 1].wait_recv()
+        solve(j)
+        settle(j)
+
+        @pl.loop(0, blocks)
+        def _(p):
+            put(p, half_front(p, j), j)
+            part_of(p, j).start()
+
+    def to_owner(slot, t):
         return pltpu.make_async_remote_copy(
-            src_ref=sbuf.at[slot], dst_ref=land.at[slot], send_sem=ss.at[slot], recv_sem=sr.at[slot],
+            src_ref=sbuf.at[slot, t], dst_ref=land.at[slot, t], send_sem=ss.at[slot, t], recv_sem=sr.at[slot, t],
             device_id=peer(slot), device_id_type=MESH,
         )
 
-    def fill(slot):
-        sbuf[slot] = summed[tab[2, slot]]
-
-    def add(p):
-        if p < EARLY:
-            part_of(p, 0).wait_recv()
-            part_of(p, 1).wait_recv()
-        else:
-            to_mate(p).wait_recv()
-        for t in range(2):
-            at = slice(t * quarter, (t + 1) * quarter)
-            summed[p, :, at] = (keep[p, :, at] + precv[p, t].astype(F32)).astype(BF16)
-        fill(p)
-
-    own = pltpu.make_async_copy(sbuf.at[HERE], land.at[HERE], ss.at[HERE])
-    for slot in range(FRONTS):
-        if slot < blocks:
-            add(slot)
-        else:
-            fill(slot)
-        if slot == HERE:
-            own.start()
-        else:
-            to_owner(slot).start()
+    owns = [pltpu.make_async_copy(sbuf.at[HERE, t], land.at[HERE, t], ss.at[HERE, t]) for t in range(2)]
+    for t in range(2):
+        for slot in range(FRONTS):
+            if slot < blocks:
+                part_of(slot, t).wait_recv()
+                summed[t, slot] = (keep[slot, t] + precv[slot, t].astype(F32)).astype(BF16)
+            sbuf[slot, t] = summed[t, tab[2, slot]]
+            if slot == HERE:
+                owns[t].start()
+            else:
+                to_owner(slot, t).start()
 
     for copy in usends + vsends:
         copy.wait_send()
-    for p in range(EARLY):
+
+    @pl.loop(0, blocks)
+    def _(p):
         part_of(p, 0).wait_send()
         part_of(p, 1).wait_send()
 
-    @pl.loop(EARLY, blocks)
-    def _(p):
-        to_mate(p).wait_send()
-
-    own.wait()
     own_mark.wait()
-
+    for t in range(2):
+        owns[t].wait()
+        for slot in others:
+            to_owner(slot, t).wait()
     for slot in others:
-        to_owner(slot).wait()
         mark(slot).wait()
 
 
@@ -288,7 +255,7 @@
     return pl.pallas_call(
         functools.partial(sketch_kernel, per_device),
         out_shape=(
-            jax.ShapeDtypeStruct((FRONTS, BLOCK, half), BF16),
+            jax.ShapeDtypeStruct((FRONTS, 2, BLOCK, half // 2), BF16),
             jax.ShapeDtypeStruct((FRONTS, 8, 128), jnp.int32),
         ),
         in_specs=[pl.BlockSpec(memory_space=pltpu.SMEM), vmem] + [hbm] * 5,
@@ -310,11 +277,11 @@
             pltpu.VMEM((2, pivot, half), F32),
             pltpu.VMEM((2, pivot, half), F32),
             pltpu.VMEM((pivot, width), BF16),
-            pltpu.VMEM((blocks, BLOCK, half), F32),
+            pltpu.VMEM((blocks, 2, BLOCK, half // 2), F32),
             pltpu.VMEM((blocks, 2, BLOCK, half // 2), BF16),
             pltpu.VMEM((blocks, 2, BLOCK, half // 2), BF16),
-            pltpu.VMEM((blocks, BLOCK, half), BF16),
-            pltpu.VMEM((FRONTS, BLOCK, half), BF16),
+            pltpu.VMEM((2, blocks, BLOCK, half // 2), BF16),
+            pltpu.VMEM((FRONTS, 2, BLOCK, half // 2), BF16),
             pltpu.SemaphoreType.DMA((8 + tiles,)),
             pltpu.SemaphoreType.DMA((4,)),
             pltpu.SemaphoreType.DMA((4,)),
@@ -322,8 +289,8 @@
             pltpu.SemaphoreType.DMA((2,)),
             pltpu.SemaphoreType.DMA((blocks, 2)),
             pltpu.SemaphoreType.DMA((blocks, 2)),
-            pltpu.SemaphoreType.DMA((FRONTS,)),
-            pltpu.SemaphoreType.DMA((FRONTS,)),
+            pltpu.SemaphoreType.DMA((FRONTS, 2)),
+            pltpu.SemaphoreType.DMA((FRONTS, 2)),
             pltpu.SemaphoreType.DMA((FRONTS,)),
             pltpu.SemaphoreType.DMA((FRONTS,)),
             pltpu.SemaphoreType.DMA,
@@ -343,6 +310,7 @@
 def parent_kernel(tags, land, basis, parent, coeff):
     parent[...] = jnp.zeros_like(parent)
     per = parent.shape[0]
+    wide = land.shape[3]
 
     @pl.loop(0, FRONTS)
     def _(slot):
@@ -350,7 +318,8 @@
 
         @pl.when(tag < per)
         def _():
-            parent[tag] += land[slot].astype(F32)
+            for t in range(2):
+                parent[tag, :, t * wide : (t + 1) * wide] += land[slot, t].astype(F32)
 
     rounded = parent[...].astype(BF16).reshape(per * BLOCK, parent.shape[2])
     coeff[...] = lax.dot_general(
@@ -360,7 +329,7 @@
 
 def parent_call(tags, land, basis):
     rows, rank = basis.shape
-    half = land.shape[2]
+    half = 2 * land.shape[3]
     vmem = pl.BlockSpec(memory_space=pltpu.VMEM)
     return pl.pallas_call(
         parent_kernel,

time: 72.5 us -> 70.5 us (0.972)
  Pallas kernels: 67 us -> 64.5 us
    pallas_call x1, Pallas kernels: 62.6 us -> 60.1 us  [sketch_call(): pl.pallas_call(functools.partial(sketch_kernel, per_device), out_shape=(j...]
where the time goes in v7:
time: 70.5 us; the launch traced here: 70.3 us
  Pallas kernels  64.5 us (91%)
  local copies, waits for them, and re-layouts  1.7 us (2%)
  waiting for transfers between devices  1.54 us (2%)
  between operations  1.32 us (2%)
  starting transfers between devices  1.12 us (2%)
    pallas_call x1, Pallas kernels, sketch_call(): pl.pallas_call(functools.partial(sketch_kernel, per_device), out_shape=(j...  60.1 us
    pallas_call x1, Pallas kernels, parent_call(): pl.pallas_call(parent_kernel, out_shape=(jax.ShapeDtypeStruct((rows // BL...  2.35 us
    pallas_call x1, Pallas kernels, residual_call(): pl.pallas_call(residual_kernel, out_shape=(jax.ShapeDtypeStruct((rows, ha...  2.1 us
    unnamed x6, local copies, waits for them, and re-layouts  1.69 us
    ppermute x1, waiting for transfers between devices, body(): other = lax.ppermute(part, 'row', [(0, 1), (1, 0)])  1.54 us
  transfers between devices with their start and end apart: 1, of which 1 were waited for; matrix products, arithmetic and copies ran while one was open for 0% of the time, Pallas kernels for 0%

profile of v7, /device:TPU:1, one launch (start us, length us, event | category | flops | bytes accessed | tf_op | source)
XLA Modules:
  0.0 70.3 jit_solution(5828567969225819808)
XLA Ops:
  1.3 0.0 copy-start.1
  1.3 1.0 %copy-done.1 = bf16[1,512,512]{2,1,0:T(8,128)(2,1)S(1)} copy-done((bf16[1,512,512]{2,1,0:T(8,128)(2,1)S(1)}, bf16[1,512,512]{2,1,0:T(8,128)(2,1)}, u32[]{:S(2)}) %copy-start.1) | copy-done | bytes 524312
  2.3 0.0 copy-start.2
  2.3 0.7 copy-done.2
  3.0 0.0 copy-start
  3.0 60.1 %sketch.1 = (bf16[32,2,128,128]{3,2,1,0:T(8,128)(2,1)S(1)}, s32[32,8,128]{2,1,0:T(8,128)S(1)}) custom-call(s32[1]{0:T(128)S(6)} %copy.10.bounds, s32[1,20]{1,0:T(1,128)S(1)} %copy-done.2, bf16[2560,512]{1,0:T(8,128)(2,1)} %sk_hbm.1, bf16[512,2560]{1,0:T(8,128)(2,1)} %bitcast.16, bf16[512,512]{1,0:T(8,128)(2,1)S(1)} %bitcast.12, ...), custom_call_target="tpu_custom_call" | custom-call | flops 10000000000 | bytes 100000000 | tf_op jit(solution)/shard_map/sketch/pallas_call | solution.py:255
  63.1 0.1 select_reduce_fusion.tags
  63.2 0.0 copy-done
  63.2 2.4 %parent.1 = (f32[24,128,256]{2,1,0:T(8,128)S(1)}, f32[512,256]{1,0:T(8,128)S(1)}) custom-call(s32[32]{0:T(128)S(1)} %select_reduce_fusion.tags, bf16[32,2,128,128]{3,2,1,0:T(8,128)(2,1)S(1)} %get-tuple-element.9.land, bf16[3072,512]{1,0:T(8,128)(2,1)S(1)} %bitcast.9), custom_call_target="tpu_custom_call" | custom-call | tf_op jit(solution)/shard_map/parent/pallas_call | solution.py:334
  65.5 1.1 %collective-permute-start = (f32[512,256]{1,0:T(8,128)S(1)}, f32[512,256]{1,0:T(8,128)S(1)}, u32[]{:S(2)}, u32[]{:S(2)}) collective-permute-start(f32[512,256]{1,0:T(8,128)S(1)} %get-tuple-element.11.part), channel_id=1, source_target_pairs={{0,2},{2,0},{1,3},{3,1},{4,6},{6,4},{5,7},{7,5},{8,10},{10,8},{9,1... | collective-permute-start | bytes 1572872 | tf_op jit(solution)/shard_map/ppermute | solution.py:399
  66.7 1.5 %collective-permute-done.other = f32[512,256]{1,0:T(8,128)S(1)} collective-permute-done((f32[512,256]{1,0:T(8,128)S(1)}, f32[512,256]{1,0:T(8,128)S(1)}, u32[]{:S(2)}, u32[]{:S(2)}) %collective-permute-start) | collective-permute-done | bytes 524320 | tf_op jit(solution)/shard_map/ppermute | solution.py:399
  68.2 2.1 %residual.1 = (f32[3072,256]{1,0:T(8,128)}, f32[512,256]{1,0:T(8,128)}) custom-call(f32[3072,256]{1,0:T(8,128)S(1)} %bitcast.11, bf16[3072,512]{1,0:T(8,128)(2,1)S(1)} %bitcast.10, f32[512,256]{1,0:T(8,128)S(1)} %get-tuple-element.11.part, f32[512,256]{1,0:T(8,128)S(1)} %collective-permute-done.other), custom_call_target="tpu_custom_call" | custom-call | tf_op jit(solution)/shard_map/residual/pallas_call | solution.py:371
  (1 shorter events, 0.0 us)
Async XLA Ops:
  1.3 1.0 %copy-start.1 = (bf16[1,512,512]{2,1,0:T(8,128)(2,1)S(1)}, bf16[1,512,512]{2,1,0:T(8,128)(2,1)}, u32[]{:S(2)}) copy-start(bf16[1,512,512]{2,1,0:T(8,128)(2,1)} %param.10) | copy-start | bytes 1572868
  2.3 0.7 copy-start.2
  3.0 60.2 %copy-start = (bf16[1,3072,512]{2,1,0:T(8,128)(2,1)S(1)}, bf16[1,3072,512]{2,1,0:T(8,128)(2,1)}, u32[]{:S(2)}) copy-start(bf16[1,3072,512]{2,1,0:T(8,128)(2,1)} %param.15) | copy-start | bytes 9437188
  65.5 2.7 %collective-permute-start = (f32[512,256]{1,0:T(8,128)S(1)}, f32[512,256]{1,0:T(8,128)S(1)}, u32[]{:S(2)}, u32[]{:S(2)}) collective-permute-start(f32[512,256]{1,0:T(8,128)S(1)} %get-tuple-element.11.part), channel_id=1, source_target_pairs={{0,2},{2,0},{1,3},{3,1},{4,6},{6,4},{5,7},{7,5},{8,10},{10,8},{9,1... | collective-permute-start | bytes 1572872 | tf_op jit(solution)/shard_map/ppermute | solution.py:399

commit v8 on v7

--- a/solution.py
+++ b/solution.py
@@ -236,12 +236,16 @@
         part_of(p, 1).wait_send()
 
     own_mark.wait()
+    for slot in others:
+        mark(slot).wait()
     for t in range(2):
         owns[t].wait()
         for slot in others:
-            to_owner(slot, t).wait()
+            to_owner(slot, t).wait_send()
+            if t == 0:
+                to_owner(slot, t).wait_recv()
     for slot in others:
-        mark(slot).wait()
+        to_owner(slot, 1).wait_recv()
 
 
 def sketch_call(per_device, bounds, block_map, sketch, upper, pinv, lower, trailing):

time: 70.5 us -> 70.3 us (level)
  no operation moved by 1% of the time
where the time goes in v8:
time: 70.3 us; the launch traced here: 70.1 us
  Pallas kernels  64.4 us (92%)
  local copies, waits for them, and re-layouts  1.7 us (2%)
  waiting for transfers between devices  1.54 us (2%)
  between operations  1.32 us (2%)
  starting transfers between devices  1.05 us (1%)
    pallas_call x1, Pallas kernels, sketch_call(): pl.pallas_call(functools.partial(sketch_kernel, per_device), out_shape=(j...  60 us
    pallas_call x1, Pallas kernels, parent_call(): pl.pallas_call(parent_kernel, out_shape=(jax.ShapeDtypeStruct((rows // BL...  2.34 us
    pallas_call x1, Pallas kernels, residual_call(): pl.pallas_call(residual_kernel, out_shape=(jax.ShapeDtypeStruct((rows, ha...  2.1 us
    unnamed x6, local copies, waits for them, and re-layouts  1.69 us
    ppermute x1, waiting for transfers between devices, body(): other = lax.ppermute(part, 'row', [(0, 1), (1, 0)])  1.54 us
  transfers between devices with their start and end apart: 1, of which 1 were waited for; matrix products, arithmetic and copies ran while one was open for 0% of the time, Pallas kernels for 0%

profile of v8, /device:TPU:1, one launch (start us, length us, event | category | flops | bytes accessed | tf_op | source)
XLA Modules:
  0.0 70.1 jit_solution(15878518994612000820)
XLA Ops:
  1.3 0.0 copy-start.1
  1.3 1.0 %copy-done.1 = bf16[1,512,512]{2,1,0:T(8,128)(2,1)S(1)} copy-done((bf16[1,512,512]{2,1,0:T(8,128)(2,1)S(1)}, bf16[1,512,512]{2,1,0:T(8,128)(2,1)}, u32[]{:S(2)}) %copy-start.1) | copy-done | bytes 524312
  2.3 0.0 copy-start.2
  2.3 0.7 copy-done.2
  3.0 0.0 copy-start
  3.0 60.0 %sketch.1 = (bf16[32,2,128,128]{3,2,1,0:T(8,128)(2,1)S(1)}, s32[32,8,128]{2,1,0:T(8,128)S(1)}) custom-call(s32[1]{0:T(128)S(6)} %copy.10.bounds, s32[1,20]{1,0:T(1,128)S(1)} %copy-done.2, bf16[2560,512]{1,0:T(8,128)(2,1)} %sk_hbm.1, bf16[512,2560]{1,0:T(8,128)(2,1)} %bitcast.16, bf16[512,512]{1,0:T(8,128)(2,1)S(1)} %bitcast.12, ...), custom_call_target="tpu_custom_call" | custom-call | flops 10000000000 | bytes 100000000 | tf_op jit(solution)/shard_map/sketch/pallas_call | solution.py:259
  63.0 0.1 select_reduce_fusion.tags
  63.1 0.0 copy-done
  63.1 2.3 %parent.1 = (f32[24,128,256]{2,1,0:T(8,128)S(1)}, f32[512,256]{1,0:T(8,128)S(1)}) custom-call(s32[32]{0:T(128)S(1)} %select_reduce_fusion.tags, bf16[32,2,128,128]{3,2,1,0:T(8,128)(2,1)S(1)} %get-tuple-element.9.land, bf16[3072,512]{1,0:T(8,128)(2,1)S(1)} %bitcast.9), custom_call_target="tpu_custom_call" | custom-call | tf_op jit(solution)/shard_map/parent/pallas_call | solution.py:338
  65.4 1.1 %collective-permute-start = (f32[512,256]{1,0:T(8,128)S(1)}, f32[512,256]{1,0:T(8,128)S(1)}, u32[]{:S(2)}, u32[]{:S(2)}) collective-permute-start(f32[512,256]{1,0:T(8,128)S(1)} %get-tuple-element.11.part), channel_id=1, source_target_pairs={{0,2},{2,0},{1,3},{3,1},{4,6},{6,4},{5,7},{7,5},{8,10},{10,8},{9,1... | collective-permute-start | bytes 1572872 | tf_op jit(solution)/shard_map/ppermute | solution.py:403
  66.5 1.5 %collective-permute-done.other = f32[512,256]{1,0:T(8,128)S(1)} collective-permute-done((f32[512,256]{1,0:T(8,128)S(1)}, f32[512,256]{1,0:T(8,128)S(1)}, u32[]{:S(2)}, u32[]{:S(2)}) %collective-permute-start) | collective-permute-done | bytes 524320 | tf_op jit(solution)/shard_map/ppermute | solution.py:403
  68.0 2.1 %residual.1 = (f32[3072,256]{1,0:T(8,128)}, f32[512,256]{1,0:T(8,128)}) custom-call(f32[3072,256]{1,0:T(8,128)S(1)} %bitcast.11, bf16[3072,512]{1,0:T(8,128)(2,1)S(1)} %bitcast.10, f32[512,256]{1,0:T(8,128)S(1)} %get-tuple-element.11.part, f32[512,256]{1,0:T(8,128)S(1)} %collective-permute-done.other), custom_call_target="tpu_custom_call" | custom-call | tf_op jit(solution)/shard_map/residual/pallas_call | solution.py:375
  (1 shorter events, 0.0 us)
Async XLA Ops:
  1.3 1.0 %copy-start.1 = (bf16[1,512,512]{2,1,0:T(8,128)(2,1)S(1)}, bf16[1,512,512]{2,1,0:T(8,128)(2,1)}, u32[]{:S(2)}) copy-start(bf16[1,512,512]{2,1,0:T(8,128)(2,1)} %param.10) | copy-start | bytes 1572868
  2.3 0.7 copy-start.2
  3.0 60.1 %copy-start = (bf16[1,3072,512]{2,1,0:T(8,128)(2,1)S(1)}, bf16[1,3072,512]{2,1,0:T(8,128)(2,1)}, u32[]{:S(2)}) copy-start(bf16[1,3072,512]{2,1,0:T(8,128)(2,1)} %param.15) | copy-start | bytes 9437188
  65.4 2.6 %collective-permute-start = (f32[512,256]{1,0:T(8,128)S(1)}, f32[512,256]{1,0:T(8,128)S(1)}, u32[]{:S(2)}, u32[]{:S(2)}) collective-permute-start(f32[512,256]{1,0:T(8,128)S(1)} %get-tuple-element.11.part), channel_id=1, source_target_pairs={{0,2},{2,0},{1,3},{3,1},{4,6},{6,4},{5,7},{7,5},{8,10},{10,8},{9,1... | collective-permute-start | bytes 1572872 | tf_op jit(solution)/shard_map/ppermute | solution.py:403
